TPU v7x, 32 devices: a whole 2x2x4 slice. The times are simulated.
32 devices in a mesh: fsdp: 32 (over z, y, x, core).
Axes of the slice: x: 2, y: 2, z: 4, core: 2. Of those that a mesh axis runs over, the one named last changes fastest.
Arguments:
- tokens: bfloat16 [32, 1024, 384], P('fsdp'), may hold values from -6 to 6
- seg_ids: int32 [32, 1024], P('fsdp'), may hold values from -1 to 19, as said below
- w_qkv: bfloat16 [442368], P('fsdp'), may hold values from -0.3125 to 0.3125
- w_out: bfloat16 [147456], P('fsdp'), may hold values from -0.875 to 0.875
- w_up: bfloat16 [589824], P('fsdp'), may hold values from -0.3125 to 0.3125
- w_down: bfloat16 [589824], P('fsdp'), may hold values from -0.15625 to 0.15625
- norm_gains: bfloat16 [768], P('fsdp'), may hold values from 0.099609375 to 1.8984375
- cotangent: bfloat16 [32, 1024, 384], P('fsdp'), may hold values from -6 to 6
Outputs:
- layer_out: bfloat16 [32, 1024, 384], P('fsdp')
- grad_tokens: float32 [32, 1024, 384], P('fsdp')
- grad_qkv: float32 [442368], P('fsdp')
- grad_out: float32 [147456], P('fsdp')
- grad_up: float32 [589824], P('fsdp')
- grad_down: float32 [589824], P('fsdp')
- grad_gains: float32 [768], P('fsdp')
Inputs may be any that keep to these rules, and one draw needn't show every extreme that they name: `seg_ids`: in each pack, slots 0 to c * 51 - 1 hold images 0 to c - 1 in consecutive runs of 51 slots, and every later slot is -1; c is 10 to 20 (at least 1), and some pack holds 20 images.
All inputs are finite; a program needn't handle non-finite values.
Results may differ from a plain program's by a relative error of at most 0.012.
Values may be sent and summed in bfloat16 or wider, within the bound.
A program may use at most 192 MiB of HBM per device.

v0:
```python
import jax
import jax.numpy as jnp
from jax import lax
from jax.sharding import PartitionSpec as P

D = 384
HEADS = 6
HEAD_DIM = 64
FF = 1536
PACK_TOK = 1024
PACKS = 1


epsilon = 1e-06
masked = -1e30


def normalize(values):
    centred = values - jnp.mean(values, axis=-1, keepdims=True)
    spread = jnp.mean(centred * centred, axis=-1, keepdims=True)
    return centred * lax.rsqrt(spread + epsilon)


def ln_gain(values, gain):
    return normalize(values) * gain


def gelu_exact(values):
    return jax.nn.gelu(values, approximate=False)


def unflatten(flat_set):
    flat_qkv, flat_out, flat_up, flat_down, flat_gains = flat_set
    return (
        flat_qkv.reshape(D, 3 * D),
        flat_out.reshape(D, D),
        flat_up.reshape(D, FF),
        flat_down.reshape(FF, D),
        flat_gains.astype(jnp.float32).reshape(2, D),
    )


def block_scores(queries, key_rows, seg_query, seg_key):
    scores = jnp.einsum(
        "qhd,khd->hqk", queries, key_rows, preferred_element_type=jnp.float32
    ) * HEAD_DIM ** (-0.5)
    same_image = seg_query[:, None] == seg_key[None, :]
    return jnp.where(same_image[None], scores, masked)


def attend_forward(qkv_pack, seg_pack):
    block_len = min(512, PACK_TOK)
    key_rows = qkv_pack[:, 1]
    value_rows = qkv_pack[:, 2]
    outputs = []
    logsums = []
    for offset in range(0, PACK_TOK, block_len):
        queries = qkv_pack[offset : offset + block_len, 0]
        scores = block_scores(queries, key_rows, seg_pack[offset : offset + block_len], seg_pack)
        row_max = jnp.max(scores, axis=2, keepdims=True)
        raised = jnp.exp(scores - row_max)
        row_total = jnp.sum(raised, axis=2, keepdims=True)
        attn_probs = (raised / row_total).astype(jnp.bfloat16)
        context = jnp.einsum(
            "hqk,khd->qhd", attn_probs, value_rows, preferred_element_type=jnp.float32
        )
        outputs.append(context.reshape(block_len, D))
        logsums.append((row_max + jnp.log(row_total))[:, :, 0])
    return (jnp.concatenate(outputs, axis=0), jnp.concatenate(logsums, axis=1))


def attend_backward(qkv_pack, seg_pack, logsum, grad_ctx_pack):
    block_len = min(512, PACK_TOK)
    scale = HEAD_DIM ** (-0.5)
    key_rows = qkv_pack[:, 1]
    value_rows = qkv_pack[:, 2]
    grad_keys = jnp.zeros((PACK_TOK, HEADS, HEAD_DIM), jnp.float32)
    grad_values = jnp.zeros((PACK_TOK, HEADS, HEAD_DIM), jnp.float32)
    grad_queries = []
    for offset in range(0, PACK_TOK, block_len):
        queries = qkv_pack[offset : offset + block_len, 0]
        grad_context = grad_ctx_pack[offset : offset + block_len]
        scores = block_scores(queries, key_rows, seg_pack[offset : offset + block_len], seg_pack)
        attn_probs = jnp.exp(scores - logsum[:, offset : offset + block_len, None])
        probs_low = attn_probs.astype(jnp.bfloat16)
        grad_probs = jnp.einsum(
            "qhd,khd->hqk", grad_context, value_rows, preferred_element_type=jnp.float32
        )
        centre = jnp.sum(grad_probs * attn_probs, axis=2, keepdims=True)
        grad_scores = (attn_probs * (grad_probs - centre)).astype(jnp.bfloat16)
        grad_queries.append(
            jnp.einsum("hqk,khd->qhd", grad_scores, key_rows, preferred_element_type=jnp.float32)
            * scale
        )
        grad_keys = (
            grad_keys
            + jnp.einsum("hqk,qhd->khd", grad_scores, queries, preferred_element_type=jnp.float32)
            * scale
        )
        grad_values = grad_values + jnp.einsum(
            "hqk,qhd->khd", probs_low, grad_context, preferred_element_type=jnp.float32
        )
    stacked = jnp.stack([jnp.concatenate(grad_queries, axis=0), grad_keys, grad_values], axis=1)
    return stacked.astype(jnp.bfloat16)


def body(tokens, seg_ids, w_qkv, w_out, w_up, w_down, norm_gains, cotangent):
    row_count = PACKS * PACK_TOK
    flat_set = (w_qkv, w_out, w_up, w_down, norm_gains)
    mat_qkv, mat_out, mat_up, mat_down, gain_pair = unflatten(
        (
            lax.all_gather(w_qkv, "fsdp", axis=0, tiled=True),
            lax.all_gather(w_out, "fsdp", axis=0, tiled=True),
            lax.all_gather(w_up, "fsdp", axis=0, tiled=True),
            lax.all_gather(w_down, "fsdp", axis=0, tiled=True),
            lax.all_gather(norm_gains, "fsdp", axis=0, tiled=True),
        )
    )
    inputs = tokens.reshape(row_count, D).astype(jnp.float32)
    normed_one = ln_gain(inputs, gain_pair[0]).astype(jnp.bfloat16)
    qkv_low = jnp.dot(normed_one, mat_qkv, preferred_element_type=jnp.float32).astype(jnp.bfloat16)
    qkv_low = qkv_low.reshape(PACKS, PACK_TOK, 3, HEADS, HEAD_DIM)
    pack_index = 0
    context, logsum = attend_forward(qkv_low[pack_index], seg_ids[pack_index])
    logsums = [logsum]
    context_low = context.astype(jnp.bfloat16)
    hidden_res = inputs + jnp.dot(context_low, mat_out, preferred_element_type=jnp.float32)
    normed_two = ln_gain(hidden_res, gain_pair[1]).astype(jnp.bfloat16)
    pre_act = jnp.dot(normed_two, mat_up, preferred_element_type=jnp.float32)
    activated = gelu_exact(pre_act).astype(jnp.bfloat16)
    layer_out = hidden_res + jnp.dot(activated, mat_down, preferred_element_type=jnp.float32)
    layer_out = layer_out.astype(jnp.bfloat16).reshape(tokens.shape)
    back_qkv, back_out, back_up, back_down, back_gains = unflatten(
        (
            lax.all_gather(flat_set[0], "fsdp", axis=0, tiled=True),
            lax.all_gather(flat_set[1], "fsdp", axis=0, tiled=True),
            lax.all_gather(flat_set[2], "fsdp", axis=0, tiled=True),
            lax.all_gather(flat_set[3], "fsdp", axis=0, tiled=True),
            lax.all_gather(flat_set[4], "fsdp", axis=0, tiled=True),
        )
    )
    grad_rows = cotangent.reshape(row_count, D)
    grad_down_mat = jnp.einsum(
        "rf,rd->fd", activated, grad_rows, preferred_element_type=jnp.float32
    )
    grad_act = jnp.einsum("rd,fd->rf", grad_rows, back_down, preferred_element_type=jnp.float32)
    gelu_pull = jax.vjp(gelu_exact, pre_act)[1]
    grad_pre = gelu_pull(grad_act)[0].astype(jnp.bfloat16)
    grad_up_mat = jnp.einsum("rd,rf->df", normed_two, grad_pre, preferred_element_type=jnp.float32)
    grad_normed_two = jnp.einsum("rf,df->rd", grad_pre, back_up, preferred_element_type=jnp.float32)
    second_pull = jax.vjp(ln_gain, hidden_res, back_gains[1])[1]
    grad_hidden_part, grad_gain_two = second_pull(grad_normed_two)
    grad_hidden = grad_rows.astype(jnp.float32) + grad_hidden_part
    grad_hidden_low = grad_hidden.astype(jnp.bfloat16)
    grad_out_mat = jnp.einsum(
        "rc,rd->cd", context_low, grad_hidden_low, preferred_element_type=jnp.float32
    )
    grad_context = jnp.einsum(
        "rd,cd->rc", grad_hidden_low, back_out, preferred_element_type=jnp.float32
    )
    grad_context = grad_context.astype(jnp.bfloat16).reshape(PACKS, PACK_TOK, HEADS, HEAD_DIM)
    pack_index = 0
    grad_qkv_parts = attend_backward(
        qkv_low[pack_index], seg_ids[pack_index], logsums[pack_index], grad_context[pack_index]
    )
    grad_qkv_rows = grad_qkv_parts.reshape(row_count, 3 * D)
    grad_qkv_mat = jnp.einsum(
        "rd,re->de", normed_one, grad_qkv_rows, preferred_element_type=jnp.float32
    )
    grad_normed_one = jnp.einsum(
        "re,de->rd", grad_qkv_rows, back_qkv, preferred_element_type=jnp.float32
    )
    first_pull = jax.vjp(ln_gain, inputs, back_gains[0])[1]
    grad_input_part, grad_gain_one = first_pull(grad_normed_one)
    grad_tokens = (grad_hidden + grad_input_part).reshape(tokens.shape)
    grad_gain_flat = jnp.concatenate([grad_gain_one, grad_gain_two], axis=0)
    shard_qkv, shard_out, shard_up, shard_down, shard_gains = (
        lax.psum_scatter(grad_qkv_mat.reshape(-1), "fsdp", scatter_dimension=0, tiled=True),
        lax.psum_scatter(grad_out_mat.reshape(-1), "fsdp", scatter_dimension=0, tiled=True),
        lax.psum_scatter(grad_up_mat.reshape(-1), "fsdp", scatter_dimension=0, tiled=True),
        lax.psum_scatter(grad_down_mat.reshape(-1), "fsdp", scatter_dimension=0, tiled=True),
        lax.psum_scatter(grad_gain_flat, "fsdp", scatter_dimension=0, tiled=True),
    )
    return (layer_out, grad_tokens, shard_qkv, shard_out, shard_up, shard_down, shard_gains)


def solution(mesh):
    return jax.shard_map(
        body,
        mesh=mesh,
        in_specs=(
            P("fsdp", None, None),
            P("fsdp", None),
            P("fsdp"),
            P("fsdp"),
            P("fsdp"),
            P("fsdp"),
            P("fsdp"),
            P("fsdp", None, None),
        ),
        out_specs=(
            P("fsdp", None, None),
            P("fsdp", None, None),
            P("fsdp"),
            P("fsdp"),
            P("fsdp"),
            P("fsdp"),
            P("fsdp"),
        ),
        check_vma=False,
    )
```

profile of v0, /device:TPU:0, one launch (start us, length us, event | category | flops | bytes accessed | tf_op | source)
XLA Modules:
  0.0 470.5 jit_solution(649892119059480698)
XLA Ops:
  9.6 42.2 %all-reduce = bf16[768]{0:T(1024)(128)(2,1)S(1)} all-reduce(bf16[768]{0:T(1024)(128)(2,1)S(1)} %dynamic-update-slice), channel_id=1, replica_groups=mesh['fsdp'=32] {'fsdp'}, use_global_device_ids=true, to_apply=%add | all-reduce | flops 768 | bytes 3072
  55.3 45.2 %all-gather = bf16[32,1,13824]{2,1,0:T(2,128)(2,1)S(1)} all-gather(bf16[1,1,13824]{2,1,0:T(2,128)(2,1)S(1)} %reshape.278), channel_id=1, replica_groups=mesh['fsdp'=32] {'fsdp'}, dimensions={0}, use_global_device_ids=true | all-gather | bytes 912384 | tf_op jit(solution)/shard_map/all_gather | solution.py:112
  100.5 6.2 %reduce.1 = bf16[32,13824]{1,0:T(8,128)(2,1)} reduce(bf16[32,1,13824]{2,1,0:T(2,128)(2,1)S(1)} %all-gather, bf16[]{:T(256)} %constant.108), dimensions={1}, to_apply=%all-gather.reduce_sub_computation | reduce | bytes 1769474 | tf_op jit(solution)/shard_map/all_gather | solution.py:112
  106.7 2.6 reshape.263
  110.3 3.0 convolution_convert_fusion
  113.4 2.9 copy.31
  119.3 2.8 fusion.1
  123.8 3.8 fusion.40
  130.0 2.8 fusion
  134.5 3.8 fusion.41
  138.3 40.9 %all-gather.1 = bf16[32,1,4608]{2,1,0:T(2,128)(2,1)} all-gather(bf16[1,1,4608]{2,1,0:T(2,128)(2,1)S(1)} %reshape.280), channel_id=1, replica_groups=mesh['fsdp'=32] {'fsdp'}, dimensions={0}, use_global_device_ids=true | all-gather | bytes 304128 | tf_op jit(solution)/shard_map/all_gather | solution.py:113
  179.2 3.4 reduce.2
  189.4 3.9 reshape.267
  193.3 18.6 %multiply_convert_fusion.2 = (bf16[1024,1536]{1,0:T(8,128)(2,1)}, f32[1024,1536]{1,0:T(8,128)}, f32[1024,1536]{1,0:T(8,128)}) fusion(bf16[384,1536]{1,0:T(8,128)(2,1)} %reshape.267, f32[1024,384]{0,1:T(8,128)} %copy-done.8, f32[384]{0:T(512)S(1)} %get-tuple-element.46, f32[1024]{0:T(1024)S(1)} %fusion.58, f32[1024]{0:T(1024)S(1)} %broadcast_multiply_fusion), kind=kOutput, calls=%fused_computation.23 | convolution fusion | flops 1311768576 | bytes 18490880 | tf_op jit(solution)/shard_map/dot_general | solution.py:129
  211.9 3.1 reshape.268
  215.0 6.8 %add_convert_fusion = bf16[1024,1536]{1,0:T(8,128)(2,1)S(1)} fusion(f32[1024,1536]{1,0:T(8,128)} %get-tuple-element.39, f32[1024,1536]{1,0:T(8,128)} %get-tuple-element.54, bf16[1536,384]{1,0:T(8,128)(2,1)} %reshape.268, bf16[1,1024,384]{2,1,0:T(8,128)(2,1)S(1)} %copy-done.23), kind=kOutput, calls=%fused_computation.22 | convolution fusion | flops 1229979648 | bytes 17694720 | tf_op jit(solution)/shard_map/rd,fd->rf/dot_general | solution.py:146
  224.1 2.9 fusion.61
  231.3 6.1 %multiply_reduce_fusion.1 = (f32[6,512]{1,0:T(8,128)S(1)}, f32[6,512,1024]{2,1,0:T(8,128)}) fusion(f32[6,512,1024]{2,1,0:T(8,128)S(1)} %bitcast.129, f32[6,512]{1,0:T(8,128)S(1)} %log_add_fusion.1, bf16[512,6,64]{0,2,1:T(8,128)(2,1)S(1)} %bitcast.142, bf16[1024,3,6,64]{0,3,2,1:T(8,128)(2,1)S(1)} %bitcast.136), kind=kOutput, calls=%fused_computation.4 | convolution fusion | flops 412087296 | bytes 26374144 | tf_op jit(solution)/shard_map/qhd,khd->hqk/dot_general | solution.py:86
  237.4 7.3 %multiply_convert_fusion.1 = bf16[6,512,1024]{2,1,0:T(8,128)(2,1)S(1)} fusion(f32[6,512,1024]{2,1,0:T(8,128)} %get-tuple-element.57, f32[6,512,1024]{2,1,0:T(8,128)S(1)} %bitcast.129, f32[6,512]{1,0:T(8,128)S(1)} %get-tuple-element.56, f32[6,512]{1,0:T(8,128)S(1)} %log_add_fusion.1), kind=kLoop, calls=%fused_computation.3 | loop fusion | flops 12582912 | bytes 31481856 | tf_op jit(solution)/shard_map/convert_element_type | solution.py:90
  244.7 2.8 fusion.43
  247.5 2.4 fusion.52
  250.0 3.2 fusion.5
  253.2 6.1 %multiply_reduce_fusion = (f32[6,512]{1,0:T(8,128)S(1)}, f32[6,512,1024]{2,1,0:T(8,128)}) fusion(f32[6,512,1024]{2,1,0:T(8,128)S(1)} %bitcast.131, f32[6,512]{1,0:T(8,128)S(1)} %log_add_fusion, bf16[512,6,64]{0,2,1:T(8,128)(2,1)S(1)} %bitcast.145, bf16[1024,3,6,64]{0,3,2,1:T(8,128)(2,1)S(1)} %bitcast.139), kind=kOutput, calls=%fused_computation.1 | convolution fusion | flops 412087296 | bytes 26374144 | tf_op jit(solution)/shard_map/qhd,khd->hqk/dot_general | solution.py:86
  259.3 3.2 fusion.46
  262.5 3.2 reshape.275
  265.8 3.2 reshape.274
  269.9 6.4 %fusion.34 = bf16[1024,1,6,64]{0,3,2,1:T(8,128)(2,1)S(1)} fusion(f32[6,64,1024]{2,1,0:T(8,128)} %fusion.5, bf16[512,6,64]{0,2,1:T(8,128)(2,1)S(1)} %bitcast.143, f32[6,512,1024]{2,1,0:T(8,128)} %copy-done, f32[6,512]{1,0:T(8,128)S(1)} %log_add_fusion.1), kind=kOutput, calls=%fused_computation.70 | convolution fusion | flops 409731072 | bytes 15347712 | tf_op jit(solution)/shard_map/hqk,qhd->khd/dot_general | solution.py:100
  276.3 9.5 %multiply_convert_fusion = bf16[6,512,1024]{2,1,0:T(8,128)(2,1)S(1)} fusion(f32[6,512,1024]{2,1,0:T(8,128)} %get-tuple-element.59, f32[6,512,1024]{2,1,0:T(8,128)} %copy-done.1, f32[6,512]{1,0:T(8,128)S(1)} %get-tuple-element.58, f32[6,512]{1,0:T(8,128)S(1)} %log_add_fusion), kind=kLoop, calls=%fused_computation | loop fusion | flops 12582912 | bytes 31481856 | tf_op jit(solution)/shard_map/convert_element_type | solution.py:90
  295.4 4.7 fusion.33
  302.4 3.4 fusion.25
  308.9 38.2 %all-reduce.5 = f32[768]{0:T(1024)S(1)} all-reduce(f32[768]{0:T(1024)S(1)} %pad_maximum_fusion.4), channel_id=6, replica_groups=mesh['fsdp'=32] {'fsdp'}, use_global_device_ids=true, to_apply=%region_20.21.clone | all-reduce | flops 768 | bytes 6144
  347.6 110.1 %all-reduce.9.cloned.1.call-done = (f32[442368]{0:T(1024)}, f32[147456]{0:T(1024)}, f32[589824]{0:T(1024)}, f32[589824]{0:T(1024)}) async-done(((f32[442368]{0:T(1024)}, f32[147456]{0:T(1024)}, f32[589824]{0:T(1024)}, f32[589824]{0:T(1024)}), (f32[442368]{0:T(1024)}, f32[147456]{0:T(1024)}, f32[589824]{0:T(1024)}, f32[589824]{0:T(1024)})) %all-reduce.9.cloned.1.call-update) | async-done | bytes 7077904
  (151 shorter events, 51.0 us)
Async XLA Ops:
  7.2 182.2 %all-gather.5.cloned.1.call-start = ((), (), s32[]{:S(2)}) async-start(), calls=%async_computation | async-start | bytes 1216512 | tf_op jit(solution)/shard_map/all_gather | solution.py:114
  7.9 204.0 %all-gather.7.cloned.1.call-start = ((), (), s32[]{:S(2)}) async-start(), calls=%async_computation.1 | async-start | bytes 1216512 | tf_op jit(solution)/shard_map/all_gather | solution.py:115
  8.6 449.1 %all-reduce.9.cloned.1.call-start = ((), (), s32[]{:S(2)}) async-start(), calls=%async_computation.2 | async-start | bytes 14155776
  51.8 57.6 %copy-start.34 = (f32[384]{0:T(512)}, f32[384]{0:T(512)S(1)}, u32[]{:S(2)}) copy-start(f32[384]{0:T(512)S(1)} %get-tuple-element.47) | copy-start | bytes 4612
  54.8 131.4 %copy-start.5 = (bf16[1,1024,384]{1,2,0:T(8,128)(2,1)}, bf16[1,1024,384]{1,2,0:T(8,128)(2,1)S(1)}, u32[]{:S(2)}) copy-start(bf16[1,1024,384]{1,2,0:T(8,128)(2,1)S(1)} %copy.30) | copy-start | bytes 2359300
  55.0 54.4 %copy-start.28 = (f32[1024]{0:T(1024)}, f32[1024]{0:T(1024)S(1)}, u32[]{:S(2)}) copy-start(f32[1024]{0:T(1024)S(1)} %broadcast_multiply_fusion.1) | copy-start | bytes 12292
  55.2 54.2 %copy-start.32 = (f32[1024]{0:T(1024)}, f32[1024]{0:T(1024)S(1)}, u32[]{:S(2)}) copy-start(f32[1024]{0:T(1024)S(1)} %fusion.24) | copy-start | bytes 12292
  55.3 54.2 %copy-start.30 = (f32[1024]{0:T(1024)}, f32[1024]{0:T(1024)S(1)}, u32[]{:S(2)}) copy-start(f32[1024]{0:T(1024)S(1)} %fusion.57) | copy-start | bytes 12292
  116.2 115.1 %copy-start.2 = (bf16[1024,1152]{0,1:T(8,128)(2,1)}, bf16[1024,1152]{0,1:T(8,128)(2,1)S(1)}, u32[]{:S(2)}) copy-start(bf16[1024,1152]{0,1:T(8,128)(2,1)S(1)} %copy.31) | copy-start | bytes 7077892
  119.3 4.5 copy-start.1
  130.0 4.5 copy-start
  134.5 3.8 copy-start.37
  193.3 21.7 %copy-start.23 = (bf16[1,1024,384]{2,1,0:T(8,128)(2,1)S(1)}, bf16[1,1024,384]{2,1,0:T(8,128)(2,1)}, u32[]{:S(2)}) copy-start(bf16[1,1024,384]{2,1,0:T(8,128)(2,1)} %param.15) | copy-start | bytes 2359300
  215.0 6.9 %copy-start.9 = (f32[1024,384]{0,1:T(8,128)S(1)}, f32[1024,384]{0,1:T(8,128)}, u32[]{:S(2)}) copy-start(f32[1024,384]{0,1:T(8,128)} %copy-done.8) | copy-start | bytes 4718596
  215.0 6.9 %copy-start.21 = (bf16[384,1536]{1,0:T(8,128)(2,1)S(1)}, bf16[384,1536]{1,0:T(8,128)(2,1)}, u32[]{:S(2)}) copy-start(bf16[384,1536]{1,0:T(8,128)(2,1)} %reshape.267) | copy-start | bytes 3538948
  221.9 9.4 %slice-start = ((s8[12582912]{0:T(1024)(128)(4,1)}), s8[4194304]{0:T(1024)(128)(4,1)S(1)}, s32[]{:S(2)}) async-start(s8[12582912]{0:T(1024)(128)(4,1)} %bitcast.128), calls=%async_computation.3 | async-start | bytes 8388608
  224.1 7.2 %slice-start.1 = ((s8[12582912]{0:T(1024)(128)(4,1)}), s8[4194304]{0:T(1024)(128)(4,1)S(1)}, s32[]{:S(2)}) async-start(s8[12582912]{0:T(1024)(128)(4,1)} %bitcast.128), calls=%async_computation.4 | async-start | bytes 8388608
  227.1 4.3 slice-start.2
  227.5 3.0 copy-start.11
  231.3 6.1 %copy-start.15 = (bf16[512,384]{0,1:T(8,128)(2,1)}, bf16[512,384]{0,1:T(8,128)(2,1)S(1)}, u32[]{:S(2)}) copy-start(bf16[512,384]{0,1:T(8,128)(2,1)S(1)} %get-tuple-element.40) | copy-start | bytes 1179652
  237.4 7.3 %copy-start.3 = (bf16[1024,1152]{0,1:T(8,128)(2,1)S(1)}, bf16[1024,1152]{0,1:T(8,128)(2,1)}, u32[]{:S(2)}) copy-start(bf16[1024,1152]{0,1:T(8,128)(2,1)} %copy-done.2) | copy-start | bytes 7077892
  237.4 12.6 %slice-start.3 = ((s8[12582912]{0:T(1024)(128)(4,1)}), s8[4194304]{0:T(1024)(128)(4,1)S(1)}, s32[]{:S(2)}) async-start(s8[12582912]{0:T(1024)(128)(4,1)} %bitcast.130), calls=%async_computation.6 | async-start | bytes 8388608
  237.4 12.6 %slice-start.4 = ((s8[12582912]{0:T(1024)(128)(4,1)}), s8[4194304]{0:T(1024)(128)(4,1)S(1)}, s32[]{:S(2)}) async-start(s8[12582912]{0:T(1024)(128)(4,1)} %bitcast.130), calls=%async_computation.7 | async-start | bytes 8388608
  244.7 5.2 %slice-start.5 = ((s8[12582912]{0:T(1024)(128)(4,1)}), s8[4194304]{0:T(1024)(128)(4,1)S(1)}, s32[]{:S(2)}) async-start(s8[12582912]{0:T(1024)(128)(4,1)} %bitcast.130), calls=%async_computation.8 | async-start | bytes 8388608
  250.0 3.2 copy-start.4
  253.2 6.1 %copy-start.24 = (bf16[1,1024,384]{2,1,0:T(8,128)(2,1)S(1)}, bf16[1,1024,384]{2,1,0:T(8,128)(2,1)}, u32[]{:S(2)}) copy-start(bf16[1,1024,384]{2,1,0:T(8,128)(2,1)} %param.15) | copy-start | bytes 2359300
  253.2 6.1 %copy-start.39 = (bf16[1024,1536]{1,0:T(8,128)(2,1)S(1)}, bf16[1024,1536]{1,0:T(8,128)(2,1)}, u32[]{:S(2)}) copy-start(bf16[1024,1536]{1,0:T(8,128)(2,1)} %get-tuple-element.38) | copy-start | bytes 9437188
  265.8 3.2 copy-start.25
  265.8 4.1 copy-start.16
  302.4 3.4 copy-start.33
  302.4 4.1 copy-start.12
  302.4 4.1 copy-start.14
  (17 other events, 28.3 us)
Sparse Core Ops, SparseCore 0:
  10.9 56.9 all-gather.4
  70.8 53.1 all-gather.6
  293.8 163.8 all-reduce.8
where the time goes:
time: 478 us; the launch traced here: 471 us
  blocking collectives  167 us (35%)
  waiting for transfers between devices  112 us (23%)
  matrix products  92.6 us (19%)
  local copies, waits for them, and re-layouts  49.2 us (10%)
  other arithmetic  35.9 us (8%)
  between operations  14.6 us (3%)
    unnamed x4, waiting for transfers between devices  112 us
    unnamed x2, blocking collectives  80.4 us
    all_gather x1, blocking collectives, body(): lax.all_gather(w_qkv, 'fsdp', axis=0, tiled=True)  45.2 us
    all_gather x1, blocking collectives, body(): lax.all_gather(w_out, 'fsdp', axis=0, tiled=True)  40.9 us
    unnamed x105, local copies, waits for them, and re-layouts  25.2 us
    dot_general x1, matrix products, body(): pre_act = jnp.dot(normed_two, mat_up, preferred_element_type=jnp.float32)  18.6 us
    convert_element_type x2, other arithmetic, attend_backward(): grad_scores = (attn_probs * (grad_probs - centre)).astype(jnp.bfloat16)  16.8 us
    dot_general x2, matrix products, attend_backward(): jnp.einsum('qhd,khd->hqk', grad_context, value_rows, preferred_element_ty...  12.2 us
  transfers between devices with their start and end apart: 3, of which 1 were waited for; matrix products, arithmetic and copies ran while one was open for 18% of the time, Pallas kernels for 0%

commit v1 on v0

v1 whole, which is shorter than its diff:
```python
import functools

import jax
import jax.numpy as jnp
from jax import lax
from jax.experimental import pallas as pl
from jax.experimental.pallas import tpu as pltpu
from jax.sharding import PartitionSpec as P

MESH = pl.DeviceIdType.MESH

f32, bf16 = jnp.float32, jnp.bfloat16
D, HEADS, HD, FF, T = 384, 6, 64, 1536, 1024
PAIRS = 3
EPS = 1e-6
NEG = -1e30
KEYS = [(0, 160), (96, 320), (240, 416), (352, 1024)] + [(496, 1024)] * 4
NN = (((1,), (0,)), ((), ()))
NT = (((1,), (1,)), ((), ()))
TN = (((0,), (0,)), ((), ()))


def dot(a, b, dims=NN):
    return lax.dot_general(a, b, dims, preferred_element_type=f32)


def norm_rows(v):
    c = v - jnp.mean(v, axis=-1, keepdims=True)
    r = lax.rsqrt(jnp.mean(c * c, axis=-1, keepdims=True) + EPS)
    return c * r, r


def norm_back(g, xhat, r):
    m1 = jnp.mean(g, axis=-1, keepdims=True)
    m2 = jnp.mean(g * xhat, axis=-1, keepdims=True)
    return (g - m1 - xhat * m2) * r


def kernel(x_ref, seg_ref, wqkv_ref, wo_ref, w1_ref, w2_ref, gain_ref, dy_ref,
           out_ref, gx_ref, gqkv_ref, gout_ref, gup_ref, gdown_ref, ggain_ref,
           xhat, rstd, a, k_p, v_p, qz, ctx, ctxt, h, rinv, b, act, du, dh, dhr, dz, dkacc, dvacc, dqkv, *es):
    G1 = gain_ref[0:1, :]
    G2 = gain_ref[1:2, :]
    R = 256
    qz[...] = jnp.zeros_like(qz)
    dz[...] = jnp.zeros_like(dz)

    def stage_a(i, _):
        rows = pl.ds(pl.multiple_of(i * R, R), R)
        n, r = norm_rows(x_ref[rows, :].astype(f32))
        xhat[rows, :] = n
        rstd[0, rows, :] = jnp.broadcast_to(r, (R, 128))
        al = (n * G1).astype(bf16)
        a[rows, :] = al
        q = dot(al, wqkv_ref[:, 0:D]).astype(bf16).astype(f32) * 0.125
        kk = dot(al, wqkv_ref[:, D:2 * D]).astype(bf16)
        vv = dot(al, wqkv_ref[:, 2 * D:]).astype(bf16)
        for p in range(PAIRS):
            k_p[p, rows, :] = kk[:, 128 * p:128 * p + 128]
            v_p[p, rows, :] = vv[:, 128 * p:128 * p + 128]
            for s in range(R // 128):
                qt = q[128 * s:128 * s + 128, 128 * p:128 * p + 128].T.astype(bf16)
                qz[p, i * (R // 128) + s, 0:64, 0:128] = qt[0:64]
                qz[p, i * (R // 128) + s, 64:128, 128:256] = qt[64:128]
        return 0

    lax.fori_loop(0, T // R, stage_a, 0)

    segf = seg_ref[0:1, :].astype(f32)
    segcol = jnp.broadcast_to(segf, (128, T)).T
    for t in range(8):
        ks, ke = KEYS[t]
        bias = jnp.where(segcol[ks:ke, :] == segf[:, 128 * t:128 * t + 128], 0.0, NEG)
        e_t = es[t]

        def att(p, _, t=t, ks=ks, ke=ke, bias=bias, e_t=e_t):
            s = dot(k_p[p, ks:ke, :], qz[p, t])
            ee, ri = [], []
            for half in range(2):
                sh = s[:, 128 * half:128 * half + 128] + bias
                m = jnp.max(sh, axis=0, keepdims=True)
                ex = jnp.exp(sh - m)
                ri.append(1.0 / jnp.sum(ex, axis=0, keepdims=True))
                ee.append(ex.astype(bf16))
            e = jnp.concatenate(ee, axis=1)
            e_t[p] = e
            rr = jnp.concatenate(ri, axis=1)
            rinv[p, t] = jnp.broadcast_to(rr, (8, 256))
            ct = dot(v_p[p, ks:ke, :], e, TN)
            ct = jnp.concatenate([ct[0:64, 0:128] * ri[0], ct[64:128, 128:256] * ri[1]], axis=0)
            lanes = pl.ds(pl.multiple_of(p * 128, 128), 128)
            ctxt[lanes, 128 * t:128 * t + 128] = ct.astype(bf16)
            ctx[128 * t:128 * t + 128, lanes] = ct.T.astype(bf16)
            return 0

        lax.fori_loop(0, PAIRS, att, 0)

    FC = 512
    def stage_d(i, gacc):
        rows = pl.ds(pl.multiple_of(i * R, R), R)
        hh = x_ref[rows, :].astype(f32) + dot(ctx[rows, :], wo_ref[...])
        n, r = norm_rows(hh)
        bl = (n * G2).astype(bf16)
        b[rows, :] = bl
        dyl = dy_ref[rows, :]
        o = hh
        db = jnp.zeros((R, D), f32)
        for c in range(FF // FC):
            cols = slice(c * FC, c * FC + FC)
            u = dot(bl, w1_ref[:, cols])
            phi = 0.5 * (1.0 + lax.erf(u * 0.7071067811865476))
            al = (u * phi).astype(bf16)
            act[rows, cols] = al
            o = o + dot(al, w2_ref[cols, :])
            gp = phi + u * jnp.exp(-0.5 * u * u) * 0.3989422804014327
            dul = (gp * dot(dyl, w2_ref[cols, :], NT)).astype(bf16)
            du[rows, cols] = dul
            db = db + dot(dul, w1_ref[:, cols], NT)
        out_ref[rows, :] = o.astype(bf16)
        gacc = gacc + jnp.sum(db * n, axis=0, keepdims=True)
        dhl = dyl.astype(f32) + norm_back(db * G2, n, r)
        dh[rows, :] = dhl
        dhrl = dhl.astype(bf16)
        dhr[rows, :] = dhrl
        dct = dot(wo_ref[...], dhrl, NT)
        for p in range(PAIRS):
            for s in range(R // 128):
                tt = i * (R // 128) + s
                ri = rinv[p, tt, 0:1, :]
                dz[p, tt, 0:64, 0:128] = (dct[128 * p:128 * p + 64, 128 * s:128 * s + 128].astype(bf16).astype(f32) * ri[:, 0:128]).astype(bf16)
                dz[p, tt, 64:128, 128:256] = (dct[128 * p + 64:128 * p + 128, 128 * s:128 * s + 128].astype(bf16).astype(f32) * ri[:, 128:256]).astype(bf16)
        return gacc

    gg2 = lax.fori_loop(0, T // R, stage_d, jnp.zeros((1, D), f32))
    ggain_ref[1:2, :] = gg2

    def w_down(i, _):
        cols = pl.ds(pl.multiple_of(i * 256, 256), 256)
        gdown_ref[cols, :] = dot(act[:, cols], dy_ref[...], TN)
        gup_ref[:, cols] = dot(b[...], du[:, cols], TN)
        return 0

    lax.fori_loop(0, FF // 256, w_down, 0)
    gout_ref[...] = dot(ctxt[...], dhr[...])

    dkacc[...] = jnp.zeros_like(dkacc)
    dvacc[...] = jnp.zeros_like(dvacc)
    for t in range(8):
        ks, ke = KEYS[t]
        e_t = es[t]

        def attb(p, _, t=t, ks=ks, ke=ke, e_t=e_t):
            dzl = dz[p, t]
            dp = dot(v_p[p, ks:ke, :], dzl)
            e = e_t[p]
            ef = e.astype(f32)
            tt = ef * dp
            c = jnp.sum(tt, axis=0, keepdims=True) * rinv[p, t, 0:1, :]
            ds = (tt - ef * c).astype(bf16)
            dvacc[p, ks:ke, :] += dot(e, dzl, NT)
            dkacc[p, ks:ke, :] += dot(ds, qz[p, t], NT)
            dqt = dot(k_p[p, ks:ke, :], ds, TN)
            dqt = jnp.concatenate([dqt[0:64, 0:128], dqt[64:128, 128:256]], axis=0) * 0.125
            lanes = pl.ds(pl.multiple_of(p * 128, 128), 128)
            dqkv[128 * t:128 * t + 128, lanes] = dqt.T.astype(bf16)
            return 0

        lax.fori_loop(0, PAIRS, attb, 0)
    for p in range(PAIRS):
        dqkv[:, D + 128 * p:D + 128 * p + 128] = dkacc[p].astype(bf16)
        dqkv[:, 2 * D + 128 * p:2 * D + 128 * p + 128] = dvacc[p].astype(bf16)

    def w_qkv(i, _):
        cols = pl.ds(pl.multiple_of(i * 384, 384), 384)
        gqkv_ref[:, cols] = dot(a[...], dqkv[:, cols], TN)
        return 0

    lax.fori_loop(0, 3, w_qkv, 0)

    def stage_g(i, gacc):
        rows = pl.ds(pl.multiple_of(i * R, R), R)
        da = dot(dqkv[rows, :], wqkv_ref[...], NT)
        n = xhat[rows, :]
        gacc = gacc + jnp.sum(da * n, axis=0, keepdims=True)
        gx_ref[rows, :] = dh[rows, :] + norm_back(da * G1, n, rstd[0, rows, 0:1])
        return gacc

    ggain_ref[0:1, :] = lax.fori_loop(0, T // R, stage_g, jnp.zeros((1, D), f32))


SCRATCH = [
    pltpu.VMEM((T, D), f32),
    pltpu.VMEM((1, T, 128), f32),
    pltpu.VMEM((T, D), bf16),
    pltpu.VMEM((PAIRS, T, 128), bf16),
    pltpu.VMEM((PAIRS, T, 128), bf16),
    pltpu.VMEM((PAIRS, 8, 128, 256), bf16),
    pltpu.VMEM((T, D), bf16),
    pltpu.VMEM((D, T), bf16),
    pltpu.VMEM((8, 128), f32),
    pltpu.VMEM((PAIRS, 8, 8, 256), f32),
    pltpu.VMEM((T, D), bf16),
    pltpu.VMEM((T, FF), bf16),
    pltpu.VMEM((T, FF), bf16),
    pltpu.VMEM((T, D), f32),
    pltpu.VMEM((T, D), bf16),
    pltpu.VMEM((PAIRS, 8, 128, 256), bf16),
    pltpu.VMEM((PAIRS, T, 128), f32),
    pltpu.VMEM((PAIRS, T, 128), f32),
    pltpu.VMEM((T, 3 * D), bf16),
] + [pltpu.VMEM((PAIRS, ke - ks, 256), bf16) for ks, ke in KEYS]


def compute(x, seg, wqkv, wo, w1, w2, gains, dy):
    vm = pl.BlockSpec(memory_space=pltpu.VMEM)
    return pl.pallas_call(
        kernel,
        out_shape=[
            jax.ShapeDtypeStruct((T, D), bf16),
            jax.ShapeDtypeStruct((T, D), f32),
            jax.ShapeDtypeStruct((D, 3 * D), f32),
            jax.ShapeDtypeStruct((D, D), f32),
            jax.ShapeDtypeStruct((D, FF), f32),
            jax.ShapeDtypeStruct((FF, D), f32),
            jax.ShapeDtypeStruct((2, D), f32),
        ],
        in_specs=[vm] * 8,
        out_specs=[vm] * 7,
        scratch_shapes=SCRATCH,
        compiler_params=pltpu.CompilerParams(vmem_limit_bytes=62 * 2**20),
        name="layer",
    )(x, seg, wqkv, wo, w1, w2, gains, dy)


ZS, KS, CS = 4, 4, 2
PAD = 16
SHAPES = ((PAD, 3 * D), (PAD, D), (PAD, FF), (48, D))


def place():
    me = lax.axis_index("fsdp")
    return me // 8, (me // 2) % 4, me % 2


def device(z, k, c):
    return ((z * 4 + k) * 2 + c,)


def greet():
    z, k, c = place()
    barrier = pltpu.get_barrier_semaphore()
    partners = [(z, k, 1 - c)] + [(z, k ^ m, c) for m in (1, 2, 3)] + [(z ^ m, k, c) for m in (1, 2, 3)]
    for p in partners:
        pl.semaphore_signal(barrier, inc=1, device_id=device(*p), device_id_type=MESH)
    pl.semaphore_wait(barrier, len(partners))


def send(src, dst, sems, i, to):
    return pltpu.make_async_remote_copy(
        src_ref=src, dst_ref=dst, send_sem=sems.at[0, i], recv_sem=sems.at[1, i],
        device_id=device(*to), device_id_type=MESH)


class Gather:
    def __init__(self, buf, sems):
        z, k, c = place()
        self.z = [send(buf.at[z, k, c], buf.at[z, k, c], sems, m - 1, (z ^ m, k, c)) for m in (1, 2, 3)]
        self.k = [send(buf.at[:, k, c], buf.at[:, k, c], sems, m + 2, (z, k ^ m, c)) for m in (1, 2, 3)]
        self.c = [send(buf.at[:, :, c], buf.at[:, :, c], sems, 6, (z, k, 1 - c))]


class Scatter:
    def __init__(self, s, rc, rp, rz, sems):
        z, k, c = place()
        self.s, self.rc, self.rp, self.rz = s, rc, rp, rz
        self.c = [send(s.at[:, :, 1 - c], rc, sems, 0, (z, k, 1 - c))]
        self.k = [send(s.at[:, k ^ m, c], rp.at[m - 1], sems, m, (z, k ^ m, c)) for m in (1, 2, 3)]
        self.z = [send(s.at[z ^ m, k, c], rz.at[m - 1], sems, m + 3, (z ^ m, k, c)) for m in (1, 2, 3)]

    def add_c(self):
        z, k, c = place()
        for i in range(ZS):
            for j in range(KS):
                self.s[i, j, c] = (self.s[i, j, c].astype(f32) + self.rc[i, j].astype(f32)).astype(bf16)

    def add_k(self):
        z, k, c = place()
        for i in range(ZS):
            t = self.s[i, k, c].astype(f32)
            for m in range(3):
                t = t + self.rp[m, i].astype(f32)
            self.s[i, k, c] = t.astype(bf16)

    def add_z(self):
        z, k, c = place()
        t = self.s[z, k, c].astype(f32)
        for m in range(3):
            t = t + self.rz[m].astype(f32)
        return t


def start(copies):
    for x in copies:
        x.start()


def wait(copies):
    for x in copies:
        x.wait()


def spread_matrix(rows, cols):
    r = lax.broadcasted_iota(jnp.int32, (rows, cols), 0)
    q = lax.broadcasted_iota(jnp.int32, (rows, cols), 1)
    at = jnp.where(r < D, r + 4 * ((r * 21846) >> 18), 16 * (r - D) + 12)
    return (at == q).astype(f32).astype(bf16)


def gain_mask():
    d = lax.broadcasted_iota(jnp.int32, (32, 2 * D), 0)
    j = lax.broadcasted_iota(jnp.int32, (32, 2 * D), 1)
    return ((j * 43691) >> 20) == d


def gain_comb():
    i = lax.broadcasted_iota(jnp.int32, (128, 2 * D), 0)
    j = lax.broadcasted_iota(jnp.int32, (128, 2 * D), 1)
    return (j - 24 * ((j * 43691) >> 20) == i).astype(f32).astype(bf16)


def gather_kernel(sq, so, su, sd, wqkv, wo, w1, w2, gains, bq, bo, bu, bd, semq, semo, semu, semd):
    z, k, c = place()
    bufs = (bq, bo, bu, bd)
    for ref, buf in zip((sq, so, su, sd), bufs):
        buf[z, k, c] = ref[...]
    greet()
    gs = [Gather(b, s) for b, s in zip(bufs, (semq, semo, semu, semd))]
    for g in gs:
        start(g.z)
    for g in gs:
        wait(g.z)
        start(g.k)
    for g in gs:
        wait(g.k)
        start(g.c)
    for g in gs:
        wait(g.c)
    u = spread_matrix(D, 512)
    wide = bq[...].reshape(512, 3 * D)
    pick = spread_matrix(D + 32, 512)[D:]
    g32 = dot(pick, wide[:, 0:128]).astype(bf16)
    gall = jnp.sum(jnp.where(gain_mask(), dot(g32, gain_comb()), 0.0), axis=0, keepdims=True)
    gains[0:1, :] = gall[:, 0:D]
    gains[1:2, :] = gall[:, D:]
    wqkv[...] = dot(u, wide).astype(bf16)
    wo[...] = dot(u, bo[...].reshape(512, D)).astype(bf16)
    w1[...] = dot(u, bu[...].reshape(512, FF)).astype(bf16)
    w2[...] = bd[...].reshape(FF, D)


def gather(sq, so, su, sd):
    vm = pl.BlockSpec(memory_space=pltpu.VMEM)
    dma = pltpu.SemaphoreType.DMA
    return pl.pallas_call(
        gather_kernel,
        out_shape=[
            jax.ShapeDtypeStruct((D, 3 * D), bf16),
            jax.ShapeDtypeStruct((D, D), bf16),
            jax.ShapeDtypeStruct((D, FF), bf16),
            jax.ShapeDtypeStruct((FF, D), bf16),
            jax.ShapeDtypeStruct((2, D), f32),
        ],
        in_specs=[vm] * 4,
        out_specs=[vm] * 5,
        scratch_shapes=[pltpu.VMEM((ZS, KS, CS) + s, bf16) for s in SHAPES] + [dma((2, 7))] * 4,
        compiler_params=pltpu.CompilerParams(collective_id=0, has_side_effects=True, vmem_limit_bytes=60 * 2**20),
        name="gather",
    )(sq, so, su, sd)


def scatter_kernel(gq, go, gu, gd, gg, oq, oo, ou, od, sq, so, su, sd, cq, co, cu, cd, pq, po, pu, pd, zq, zo, zu, zd,
                   semq, semo, semu, semd):
    greet()
    ut = spread_matrix(D + 32, 512)
    grow = jnp.concatenate([gg[0:1, :], gg[1:2, :]], axis=1)
    grow = jnp.where(gain_mask(), jnp.broadcast_to(grow, (32, 2 * D)), 0.0).astype(bf16)
    grow = dot(grow, gain_comb(), NT).astype(bf16)
    gqb = gq[...].astype(bf16)
    full = jnp.concatenate([gqb, jnp.concatenate([grow, jnp.zeros((32, 3 * D - 128), bf16)], axis=1)], axis=0)
    sq[...] = dot(ut, full, TN).astype(bf16).reshape(sq.shape)
    so[...] = dot(ut[0:D], go[...].astype(bf16), TN).astype(bf16).reshape(so.shape)
    su[...] = dot(ut[0:D], gu[...].astype(bf16), TN).astype(bf16).reshape(su.shape)
    sd[...] = gd[...].astype(bf16).reshape(sd.shape)
    ss = [
        Scatter(sd, cd, pd, zd, semd),
        Scatter(su, cu, pu, zu, semu),
        Scatter(so, co, po, zo, semo),
        Scatter(sq, cq, pq, zq, semq),
    ]
    for s in ss:
        start(s.c)
    for s in ss:
        wait(s.c)
        s.add_c()
        start(s.k)
    for s in ss:
        wait(s.k)
        s.add_k()
        start(s.z)
    for s, o in zip(ss, (od, ou, oo, oq)):
        wait(s.z)
        o[...] = s.add_z()


def scatter(gq, go, gu, gd, gg):
    vm = pl.BlockSpec(memory_space=pltpu.VMEM)
    dma = pltpu.SemaphoreType.DMA
    return pl.pallas_call(
        scatter_kernel,
        out_shape=[jax.ShapeDtypeStruct(s, f32) for s in SHAPES],
        in_specs=[vm] * 5,
        out_specs=[vm] * 4,
        scratch_shapes=[pltpu.VMEM((ZS, KS, CS) + s, bf16) for s in SHAPES]
        + [pltpu.VMEM((ZS, KS) + s, bf16) for s in SHAPES]
        + [pltpu.VMEM((3, ZS) + s, bf16) for s in SHAPES]
        + [pltpu.VMEM((3,) + s, bf16) for s in SHAPES]
        + [dma((2, 7))] * 4,
        compiler_params=pltpu.CompilerParams(collective_id=1, has_side_effects=True, vmem_limit_bytes=60 * 2**20),
        name="scatter",
    )(gq, go, gu, gd, gg)


def pad_rows(m):
    return jnp.pad(m, ((0, PAD - m.shape[0]), (0, 0)))


def body_direct(tokens, seg_ids, w_qkv, w_out, w_up, w_down, norm_gains, cotangent):
    gain_row = jnp.pad(norm_gains, (0, 3 * D - norm_gains.shape[0])).reshape(1, 3 * D)
    sq = pad_rows(jnp.concatenate([w_qkv.reshape(-1, 3 * D), gain_row], axis=0))
    so = pad_rows(w_out.reshape(-1, D))
    su = pad_rows(w_up.reshape(-1, FF))
    wqkv, wo, w1, w2, gains = gather(sq, so, su, w_down.reshape(-1, D))
    out, gx, gq, go, gu, gd, gg = compute(tokens[0], seg_ids, wqkv, wo, w1, w2, gains, cotangent[0])
    oq, oo, ou, od = scatter(gq, go, gu, gd, gg)
    return (out[None], gx[None], oq[:12].reshape(-1), oo[:12].reshape(-1), ou[:12].reshape(-1), od.reshape(-1),
            oq[12, :24])


def body_plain(tokens, seg_ids, w_qkv, w_out, w_up, w_down, norm_gains, cotangent):
    whole = [lax.all_gather(w, "fsdp", axis=0, tiled=True) for w in (w_qkv, w_out, w_up, w_down, norm_gains)]
    out, gx, *grads = compute(
        tokens[0], seg_ids, whole[0].reshape(D, 3 * D), whole[1].reshape(D, D), whole[2].reshape(D, FF),
        whole[3].reshape(FF, D), whole[4].astype(f32).reshape(2, D), cotangent[0])
    shards = [lax.psum_scatter(g.reshape(-1), "fsdp", scatter_dimension=0, tiled=True) for g in grads]
    return (out[None], gx[None], *shards)


def solution(mesh):
    direct = mesh.shape["fsdp"] == ZS * KS * CS
    rows, flat = P("fsdp", None, None), P("fsdp")
    return jax.shard_map(
        body_direct if direct else body_plain,
        mesh=mesh,
        in_specs=(rows, P("fsdp", None), flat, flat, flat, flat, flat, rows),
        out_specs=(rows, rows, flat, flat, flat, flat, flat),
        check_vma=False,
    )
```

time: 478 us -> 156 us (0.33); the launches traced: 471 us -> 155 us
  blocking collectives: 167 us -> 0 us
  Pallas kernels: 0 us -> 141 us
  waiting for transfers between devices: 112 us -> 0 us
  matrix products: 92.6 us -> 0 us
  local copies, waits for them, and re-layouts: 49.2 us -> 12.8 us
  other arithmetic: 35.9 us -> 0.63 us
  between operations: 14.6 us -> 0.66 us
    pallas_call x0 -> x3, Pallas kernels: none -> 141 us  [the longest x1 59.2 us: compute(): pl.pallas_call(kernel, out_shape=[jax.ShapeDtypeStruct((T, D), bf16), jax...]
    unnamed x4 -> x0, waiting for transfers between devices: 112 us -> none
    dot_general x24 -> x0, matrix products: 92.6 us -> none  [the longest x1 18.6 us: body(): pre_act = jnp.dot(normed_two, mat_up, preferred_element_type=jnp.float32)]
    all_gather x2 -> x0, blocking collectives: 86.1 us -> none  [the longest x1 45.2 us: body(): lax.all_gather(w_qkv, 'fsdp', axis=0, tiled=True)]
    unnamed x2 -> x0, blocking collectives: 80.4 us -> none
    unnamed x105 -> x0, local copies, waits for them, and re-layouts: 25.2 us -> none
    convert_element_type x3 -> x0, other arithmetic: 17.1 us -> none  [the longest x2 16.8 us: attend_backward(): grad_scores = (attn_probs * (grad_probs - centre)).astype(jnp.bfloat16)]
    reshape x8 -> x9, local copies, waits for them, and re-layouts: 19.6 us -> 9.69 us  [the longest x1 1.53 us: body_direct(): ou[:12].reshape(-1)]
  transfers between devices with their start and end apart: 3 -> 0, of which waited for: 1 -> 0; matrix products, arithmetic and copies ran while one was open for 18% -> 0% of each run, Pallas kernels for 0% -> 0%
where the time goes in v1:
time: 156 us; the launch traced here: 155 us
  Pallas kernels  141 us (90%)
  local copies, waits for them, and re-layouts  12.8 us (8%)
    pallas_call x1, Pallas kernels, compute(): pl.pallas_call(kernel, out_shape=[jax.ShapeDtypeStruct((T, D), bf16), jax...  59.2 us
    pallas_call x1, Pallas kernels, scatter(): pl.pallas_call(scatter_kernel, out_shape=[jax.ShapeDtypeStruct(s, f32) fo...  41.3 us
    pallas_call x1, Pallas kernels, gather(): pl.pallas_call(gather_kernel, out_shape=[jax.ShapeDtypeStruct((D, 3 * D),...  40.5 us

profile of v1, /device:TPU:0, one launch (start us, length us, event | category | flops | bytes accessed | tf_op | source)
XLA Modules:
  0.0 155.1 jit_solution(5673753985066034100)
XLA Ops:
  0.6 0.7 pad.16
  1.3 0.7 reshape.43
  2.0 0.6 pad.18.so
  2.6 0.8 reshape.41
  3.4 0.6 fusion.2.sq
  4.1 1.4 reshape.45.sd
  5.5 0.8 reshape.44
  6.3 0.6 pad.19.su
  7.0 40.5 %gather.1 = (bf16[384,1152]{1,0:T(8,128)(2,1)}, bf16[384,384]{1,0:T(8,128)(2,1)}, bf16[384,1536]{1,0:T(8,128)(2,1)}, bf16[1536,384]{1,0:T(8,128)(2,1)}, f32[2,384]{1,0:T(2,128)}) custom-call(bf16[16,1152]{1,0:T(8,128)(2,1)} %fusion.2.sq, bf16[16,384]{1,0:T(8,128)(2,1)} %pad.18.so, bf16[16,1536]{1,0:T(8,128)(2,1)} %pad.19.su, bf16[48,384]{1,0:T(8,128)(2,1)} %reshape.45.sd), custom_call_target="tpu_custom_call" | custom-call | tf_op jit(solution)/shard_map/gather/pallas_call | solution.py:364
  47.5 59.2 %layer.1 = (bf16[1024,384]{1,0:T(8,128)(2,1)}, f32[1024,384]{1,0:T(8,128)}, f32[384,1152]{1,0:T(8,128)}, f32[384,384]{1,0:T(8,128)}, f32[384,1536]{1,0:T(8,128)}, /*index=5*/f32[1536,384]{1,0:T(8,128)}, f32[2,384]{1,0:T(2,128)}) custom-call(bf16[1024,384]{1,0:T(8,128)(2,1)} %bitcast.9, s32[1,1024]{1,0:T(1,128)} %seg_ref.1, ...), custom_call_target="tpu_custom_call" | custom-call | tf_op jit(solution)/shard_map/layer/pallas_call | solution.py:216
  106.7 41.3 %scatter.1 = (f32[16,1152]{1,0:T(8,128)}, f32[16,384]{1,0:T(8,128)}, f32[16,1536]{1,0:T(8,128)}, f32[48,384]{1,0:T(8,128)}) custom-call(f32[384,1152]{1,0:T(8,128)} %get-tuple-element.30.gq, f32[384,384]{1,0:T(8,128)} %get-tuple-element.31.go, f32[384,1536]{1,0:T(8,128)} %get-tuple-element.32.gu, f32[1536,384]{1,0:T(8,128)} %get-tuple-element.33.gd, ...), custom_call_target="tpu_custom_call" | custom-call | tf_op jit(solution)/shard_map/scatter/pallas_call | solution.py:418
  148.0 1.3 reshape.47
  149.3 1.5 reshape.48
  150.9 1.2 slice_bitcast_fusion
  152.1 1.5 reshape.46
  153.6 1.5 reshape.49
  (1 shorter events, 0.0 us)

commit v2 on v1

v2 whole, which is shorter than its diff:
```python
import functools

import jax
import jax.numpy as jnp
from jax import lax
from jax.experimental import pallas as pl
from jax.experimental.pallas import tpu as pltpu
from jax.sharding import PartitionSpec as P

MESH = pl.DeviceIdType.MESH
f32, bf16 = jnp.float32, jnp.bfloat16
D, HEADS, HD, FF, T = 384, 6, 64, 1536, 1024
PAIRS, TILES = 3, 8
EPS = 1e-6
NEG = -1e30
HALF = FF // 2
PAD = 16
KEYS = [(0, 160), (96, 320), (240, 416), (352, 1024)] + [(496, 1024)] * 4
NN = (((1,), (0,)), ((), ()))
NT = (((1,), (1,)), ((), ()))
TN = (((0,), (0,)), ((), ()))
DEVICES = 32


def dot(a, b, dims=NN):
    return lax.dot_general(a, b, dims, preferred_element_type=f32)


def norm_rows(v):
    c = v - jnp.mean(v, axis=-1, keepdims=True)
    r = lax.rsqrt(jnp.mean(c * c, axis=-1, keepdims=True) + EPS)
    return c * r, r


def norm_back(g, xhat, r):
    m1 = jnp.mean(g, axis=-1, keepdims=True)
    m2 = jnp.mean(g * xhat, axis=-1, keepdims=True)
    return (g - m1 - xhat * m2) * r


def spread_matrix(rows, cols):
    r = lax.broadcasted_iota(jnp.int32, (rows, cols), 0)
    q = lax.broadcasted_iota(jnp.int32, (rows, cols), 1)
    at = jnp.where(r < D, r + 4 * ((r * 21846) >> 18), 16 * (r - D) + 12)
    return (at == q).astype(f32).astype(bf16)


def gain_mask():
    d = lax.broadcasted_iota(jnp.int32, (32, 2 * D), 0)
    j = lax.broadcasted_iota(jnp.int32, (32, 2 * D), 1)
    return ((j * 43691) >> 20) == d


def gain_comb():
    i = lax.broadcasted_iota(jnp.int32, (128, 2 * D), 0)
    j = lax.broadcasted_iota(jnp.int32, (128, 2 * D), 1)
    return (j - 24 * ((j * 43691) >> 20) == i).astype(f32).astype(bf16)


BOX = (2, 2, 2, 2, 2)


def place():
    me = lax.axis_index("fsdp")
    return me // 8, (me // 4) % 2, (me // 2) % 2, me % 2


def device(z, y, x, c):
    return (((z * 2 + y) * 2 + x) * 2 + c,)


class Copy:
    def __init__(self, *args):
        self.args = args

    def make(self):
        src, dst, sems, i, to = self.args
        return pltpu.make_async_remote_copy(
            src_ref=src, dst_ref=dst, send_sem=sems.at[0, i], recv_sem=sems.at[1, i],
            device_id=device(*to), device_id_type=MESH)

    def start(self):
        self.make().start()

    def wait(self):
        self.make().wait()


send = Copy


def greet():
    z, y, x, c = place()
    barrier = pltpu.get_barrier_semaphore()
    partners = [(z, y, x, 1 - c), (z, y, 1 - x, c), (z, 1 - y, x, c), (z, 1 - y, 1 - x, c)]
    partners += [(z ^ m, y, x, c) for m in (1, 2, 3)]
    for p in partners:
        pl.semaphore_signal(barrier, inc=1, device_id=device(*p), device_id_type=MESH)
    pl.semaphore_wait(barrier, len(partners))


def start(copies):
    for q in copies:
        q.start()


def wait(copies):
    for q in copies:
        q.wait()


def gather_steps(b, sems, split):
    z, y, x, c = place()
    zh, zl = z // 2, z % 2
    own = b.at[zh, zl, y, x, c]
    line = [send(own, own, sems, m - 1, (z ^ m, y, x, c)) for m in (1, 2, 3)]
    col = b.at[:, :, y, x, c]
    near = [send(col, col, sems, 3, (z, y, 1 - x, c)), send(col, col, sems, 4, (z, 1 - y, x, c))]
    core = [send(b.at[:, :, :, :, c], b.at[:, :, :, :, c], sems, 7, (z, y, x, 1 - c))]
    if not split:
        far = [send(col, col, sems, 5, (z, 1 - y, 1 - x, c))]
        return [line, near + far, core]
    fx, fy = b.at[:, 0, y, 1 - x, c], b.at[:, 1, 1 - y, x, c]
    far = [send(fx, fx, sems, 5, (z, 1 - y, x, c)), send(fy, fy, sems, 6, (z, y, 1 - x, c))]
    return [line, near, far, core]


class Scatter:
    def __init__(self, s, rc, rx, ry, sx, sy, sems, h=pl.ds(0, 2), nh=2):
        z, y, x, c = place()
        self.s, self.rc, self.rx, self.ry, self.sx, self.sy, self.h0, self.nh = s, rc, rx, ry, sx, sy, h.start, nh
        self.core = [send(s.at[h, :, :, :, 1 - c], rc.at[h], sems, 0, (z, y, x, 1 - c))]
        self.near = [
            send(s.at[h, 0, :, 1 - x, c], rx.at[h], sems, 1, (z, y, 1 - x, c)),
            send(s.at[h, 1, 1 - y, :, c], ry.at[h], sems, 2, (z, 1 - y, x, c)),
        ]
        self.far = [
            send(s.at[h, 0, 1 - y, x, c], sy.at[h], sems, 3, (z, 1 - y, x, c)),
            send(s.at[h, 1, y, 1 - x, c], sx.at[h], sems, 4, (z, y, 1 - x, c)),
        ]

    def add_core(self):
        z, y, x, c = place()
        s, rc = self.s, self.rc
        for i in range(self.h0, self.h0 + self.nh):
            for j in range(2):
                for k in range(2):
                    for l in range(2):
                        s[i, j, k, l, c] = (s[i, j, k, l, c].astype(f32) + rc[i, j, k, l].astype(f32)).astype(bf16)

    def add_near(self):
        z, y, x, c = place()
        s = self.s
        for i in range(self.h0, self.h0 + self.nh):
            s[i, 0, 1 - y, x, c] = (s[i, 0, 1 - y, x, c].astype(f32) + self.rx[i, 1 - y].astype(f32)).astype(bf16)
            s[i, 1, y, 1 - x, c] = (s[i, 1, y, 1 - x, c].astype(f32) + self.ry[i, 1 - x].astype(f32)).astype(bf16)

    def add_far(self):
        z, y, x, c = place()
        s = self.s
        for i in range(self.h0, self.h0 + self.nh):
            s[i, 0, y, x, c] = (s[i, 0, y, x, c].astype(f32) + self.rx[i, y].astype(f32)
                                + self.sy[i].astype(f32)).astype(bf16)
            s[i, 1, y, x, c] = (s[i, 1, y, x, c].astype(f32) + self.ry[i, x].astype(f32)
                                + self.sx[i].astype(f32)).astype(bf16)

    def core_to_near(self):
        wait(self.core)
        self.add_core()
        start(self.near)

    def near_to_far(self):
        wait(self.near)
        self.add_near()
        start(self.far)

    def end_far(self):
        wait(self.far)
        self.add_far()


def line_steps(s, rz, sems):
    z, y, x, c = place()
    return [send(s.at[(z ^ m) // 2, (z ^ m) % 2, y, x, c], rz.at[m - 1], sems, m + 4, (z ^ m, y, x, c))
            for m in (1, 2, 3)]


def line_sum(s, rz):
    z, y, x, c = place()
    return s[z // 2, z % 2, y, x, c].astype(f32) + rz[0].astype(f32) + rz[1].astype(f32) + rz[2].astype(f32)


def layer_kernel(
    x_ref, seg_ref, fq, fo, fu, fd, fg, dy_ref,
    out_hbm, gx_hbm, oq, oo, ou, od, og,
    bq, bo, bu, bd, u512, wqkv, wo, w1, w2, gains, flat, sf,
    xhat, rstd, a, k_p, v_p, qz, ctx, ctxt, rinv, hhat, rstd2, b, act, du, oacc, dbacc, out_v, dh, dhr, dz,
    dkacc, dvacc, dqkv, es, biases,
    sq, so, su, sd, cq, co, cu, cd, xq, xo, xu, xd, yq, yo, yu, yd, vq, vo, vu, vd, hq, ho, hu, hd, zq, zo, zu, zd,
    gsem, ssem, lsem,
):
    z, y, x, c = place()
    zh, zl = z // 2, z % 2

    sf[...] = jnp.zeros_like(sf)

    def to_slot(src, width, rows, dst, cols):
        n = rows * width
        flat[0:n, :] = src[...].astype(f32)
        for j in range(width):
            if rows == 12:
                sf[0:12, :] = flat[pl.ds(j, rows, stride=width), :]
                piece = sf[...]
            else:
                piece = flat[pl.ds(j, rows, stride=width), :]
            dref, cj = dst(j) if callable(dst) else (dst, j)
            dref[zh, zl, y, x, c, :, 128 * cj:128 * cj + 128] = piece.astype(bf16)

    to_slot(fq, 9, 12, lambda j: (bq.at[j % 3], j // 3), None)
    sf[12:13, 0:24] = fg[...].astype(f32)
    sf[0:12, :] = flat[pl.ds(0, 12, stride=9), :]
    bq[0, zh, zl, y, x, c, :, 0:128] = sf[...].astype(bf16)
    sf[...] = jnp.zeros_like(sf)
    greet()
    gq = [gather_steps(bq.at[p], gsem.at[p], False) for p in range(PAIRS)]
    start(gq[0][0])
    start(gq[1][0])
    start(gq[2][0])
    to_slot(fo, 3, 12, bo, None)
    to_slot(fu, 12, 12, bu, None)
    to_slot(fd, 3, 48, bd, None)
    go = gather_steps(bo, gsem.at[3], True)
    gu = gather_steps(bu, gsem.at[4], True)
    gd = gather_steps(bd, gsem.at[5], True)

    u512[...] = spread_matrix(D + 32, 512)
    qz[...] = jnp.zeros_like(qz)
    dz[...] = jnp.zeros_like(dz)

    def norm_in(i, _):
        rows = pl.ds(pl.multiple_of(i * 256, 256), 256)
        n, r = norm_rows(x_ref[rows, :].astype(f32))
        xhat[rows, :] = n
        rstd[rows, :] = jnp.broadcast_to(r, (256, 128))
        return 0

    lax.fori_loop(0, T // 256, norm_in, 0)
    segf = seg_ref[0:1, :].astype(f32)
    segcol = jnp.broadcast_to(segf, (128, T)).T
    for t in range(TILES):
        ks, ke = KEYS[t]
        biases[t][...] = jnp.where(segcol[ks:ke, :] == segf[:, 128 * t:128 * t + 128], 0.0, NEG)

    wait(gq[0][0])
    start(gq[0][1])
    wait(gq[1][0])
    start(gq[1][1])
    wait(gq[2][0])
    start(gq[2][1])
    start(go[0])
    start(gu[0])
    start(gd[0])
    wait(gq[0][1])
    start(gq[0][2])
    wait(gq[0][2])

    wide = bq[0, ..., 0:128].reshape(512, 128)
    g32 = dot(u512[D:, :], wide).astype(bf16)
    gall = jnp.sum(jnp.where(gain_mask(), dot(g32, gain_comb()), 0.0), axis=0, keepdims=True)
    gains[0:1, :] = gall[:, 0:D]
    gains[1:2, :] = gall[:, D:]
    G1 = gains[0:1, :]
    G2 = gains[1:2, :]
    a[...] = (xhat[...] * G1).astype(bf16)

    def forward_pair(p, _):
        lanes = pl.ds(pl.multiple_of(p * 128, 128), 128)

        @pl.when(p > 0)
        def _():
            wait(gather_steps(bq.at[p], gsem.at[p], False)[2])

        w = dot(u512[0:D, :], bq[p].reshape(512, D)).astype(bf16)
        for j in range(3):
            wqkv[:, pl.ds(pl.multiple_of(j * D + p * 128, 128), 128)] = w[:, 128 * j:128 * j + 128]
        for i in range(2):
            rows = slice(512 * i, 512 * i + 512)
            qkv = dot(a[rows, :], w)
            q = qkv[:, 0:128].astype(bf16).astype(f32) * 0.125
            k_p[p, rows, :] = qkv[:, 128:256].astype(bf16)
            v_p[p, rows, :] = qkv[:, 256:384].astype(bf16)
            for s in range(4):
                qt = q[128 * s:128 * s + 128, :].T.astype(bf16)
                qz[p, 4 * i + s, 0:64, 0:128] = qt[0:64]
                qz[p, 4 * i + s, 64:128, 128:256] = qt[64:128]

        @pl.when(p == 0)
        def _():
            wait(gq[1][1])
            start(gq[1][2])
            wait(gq[2][1])
            start(gq[2][2])
            wait(go[0])
            start(go[1])
            wait(gu[0])
            start(gu[1])
            wait(gd[0])
            start(gd[1])

        @pl.when(p == 1)
        def _():
            wait(go[1])
            start(go[2])
            wait(gu[1])
            start(gu[2])

        @pl.when(p == 2)
        def _():
            wait(gd[1])
            start(gd[2])
            wait(go[2])
            start(go[3])
            wait(gu[2])
            start(gu[3])

        for t in range(TILES):
            ks, ke = KEYS[t]
            s = dot(k_p[p, ks:ke, :], qz[p, t])
            ee, ri = [], []
            for half in range(2):
                sh = s[:, 128 * half:128 * half + 128] + biases[t][...]
                m = jnp.max(sh, axis=0, keepdims=True)
                ex = jnp.exp(sh - m)
                ri.append(1.0 / jnp.sum(ex, axis=0, keepdims=True))
                ee.append(ex.astype(bf16))
            e = jnp.concatenate(ee, axis=1)
            es[t][p] = e
            rr = jnp.concatenate(ri, axis=1)
            rinv[p, t] = jnp.broadcast_to(rr, (8, 256))
            ct = dot(v_p[p, ks:ke, :], e, TN)
            ct = jnp.concatenate([ct[0:64, 0:128] * ri[0], ct[64:128, 128:256] * ri[1]], axis=0)
            ctxt[lanes, 128 * t:128 * t + 128] = ct.astype(bf16)
            ctx[128 * t:128 * t + 128, lanes] = ct.T.astype(bf16)
        return 0

    lax.fori_loop(0, PAIRS, forward_pair, 0)

    wait(gd[2])
    start(gd[3])
    wait(go[3])
    wo[...] = dot(u512[0:D, :], bo[...].reshape(512, D)).astype(bf16)
    for i in range(2):
        rows = slice(512 * i, 512 * i + 512)
        hh = x_ref[rows, :].astype(f32) + dot(ctx[rows, :], wo[...])
        n, r = norm_rows(hh)
        hhat[rows, :] = n
        rstd2[rows, :] = jnp.broadcast_to(r, (512, 128))
        b[rows, :] = (n * G2).astype(bf16)
        oacc[rows, :] = hh
    wait(gu[3])
    w1[...] = dot(u512[0:D, :], bu[...].reshape(512, FF)).astype(bf16)
    wait(gd[3])
    w2[...] = bd[...].reshape(FF, D)

    rs_u = [Scatter(su.at[j], cu.at[j], xu.at[j], yu.at[j], vu.at[j], hu.at[j], ssem.at[j]) for j in range(2)]
    rs_d = [Scatter(sd, cd, xd, yd, vd, hd, ssem.at[2 + j], pl.ds(j, 1), 1) for j in range(2)]
    rs_o = Scatter(so, co, xo, yo, vo, ho, ssem.at[4])
    ln_u = [line_steps(su.at[j], zu.at[j], ssem.at[j]) for j in range(2)]
    ln_d = line_steps(sd, zd, ssem.at[2])
    ln_o = line_steps(so, zo, ssem.at[4])

    for j in range(2):
        cols = slice(HALF * j, HALF * j + HALF)
        for i in range(2):
            rows = slice(512 * i, 512 * i + 512)
            u = dot(b[rows, :], w1[:, cols])
            phi = 0.5 * (1.0 + lax.erf(u * 0.7071067811865476))
            al = (u * phi).astype(bf16)
            act[rows, :] = al
            oacc[rows, :] += dot(al, w2[cols, :])
            gp = phi + u * jnp.exp(-0.5 * u * u) * 0.3989422804014327
            dul = (gp * dot(dy_ref[rows, :], w2[cols, :], NT)).astype(bf16)
            du[rows, :] = dul
            db = dot(dul, w1[:, cols], NT)
            if j == 0:
                dbacc[rows, :] = db
            else:
                dbacc[rows, :] += db
            if j == 1:
                if i == 0:
                    rs_d[0].core_to_near()
                    rs_u[0].core_to_near()
                else:
                    rs_d[0].near_to_far()
                    rs_u[0].near_to_far()
        sd[j] = dot(act[...], dy_ref[...], TN).astype(bf16).reshape((2, 2, 2, 2, 48, D))
        start(rs_d[j].core)
        gup = dot(b[...], du[...], TN).astype(bf16)
        su[j] = dot(u512[0:D, :], gup, TN).astype(bf16).reshape(BOX + (PAD, HALF))
        start(rs_u[j].core)

    out_v[...] = oacc[...].astype(bf16)
    out_copy = pltpu.make_async_copy(out_v, out_hbm, lsem.at[0])
    out_copy.start()
    rs_d[0].end_far()
    rs_u[0].end_far()
    start(ln_u[0])
    gg2 = jnp.zeros((1, D), f32)
    for i in range(2):
        rows = slice(512 * i, 512 * i + 512)
        n = hhat[rows, :]
        db = dbacc[rows, :]
        gg2 = gg2 + jnp.sum(db * n, axis=0, keepdims=True)
        dhl = dy_ref[rows, :].astype(f32) + norm_back(db * G2, n, rstd2[rows, 0:1])
        dh[rows, :] = dhl
        dhrl = dhl.astype(bf16)
        dhr[rows, :] = dhrl
        dct = dot(wo[...], dhrl, NT)
        for p in range(PAIRS):
            for s in range(4):
                t = 4 * i + s
                ri = rinv[p, t, 0:1, :]
                top = dct[128 * p:128 * p + 64, 128 * s:128 * s + 128].astype(bf16).astype(f32)
                low = dct[128 * p + 64:128 * p + 128, 128 * s:128 * s + 128].astype(bf16).astype(f32)
                dz[p, t, 0:64, 0:128] = (top * ri[:, 0:128]).astype(bf16)
                dz[p, t, 64:128, 128:256] = (low * ri[:, 128:256]).astype(bf16)
    gout = dot(ctxt[...], dhr[...]).astype(bf16)
    so[...] = dot(u512[0:D, :], gout, TN).astype(bf16).reshape(BOX + (PAD, D))
    start(rs_o.core)
    rs_d[1].core_to_near()
    rs_u[1].core_to_near()

    dkacc[...] = jnp.zeros_like(dkacc)
    dvacc[...] = jnp.zeros_like(dvacc)

    def rs_q(p):
        return Scatter(sq.at[p], cq.at[p], xq.at[p], yq.at[p], vq.at[p], hq.at[p], ssem.at[5 + p])

    def ln_q(p):
        return line_steps(sq.at[p], zq.at[p], ssem.at[5 + p])

    def backward_pair(p, gg1):
        lanes = pl.ds(pl.multiple_of(p * 128, 128), 128)
        for t in range(TILES):
            ks, ke = KEYS[t]
            dzl = dz[p, t]
            dp = dot(v_p[p, ks:ke, :], dzl)
            e = es[t][p]
            ef = e.astype(f32)
            tt = ef * dp
            cc = jnp.sum(tt, axis=0, keepdims=True) * rinv[p, t, 0:1, :]
            ds = (tt - ef * cc).astype(bf16)
            dvacc[p, ks:ke, :] += dot(e, dzl, NT)
            dkacc[p, ks:ke, :] += dot(ds, qz[p, t], NT)
            dqt = dot(k_p[p, ks:ke, :], ds, TN)
            dqt = jnp.concatenate([dqt[0:64, 0:128], dqt[64:128, 128:256]], axis=0) * 0.125
            dqkv[p, 128 * t:128 * t + 128, 0:128] = dqt.T.astype(bf16)
        dqkv[p, :, 128:256] = dkacc[p].astype(bf16)
        dqkv[p, :, 256:384] = dvacc[p].astype(bf16)
        g = dot(a[...], dqkv[p], TN)
        for j in range(3):
            wj = wqkv[:, pl.ds(pl.multiple_of(j * D + p * 128, 128), 128)].astype(f32)
            gg1 = gg1 + wj * g[:, 128 * j:128 * j + 128]
        gsum = jnp.sum(gg1.T, axis=0, keepdims=True) / G1
        grow = jnp.concatenate([gsum, gg2], axis=1)
        grow = jnp.where(gain_mask(), jnp.broadcast_to(grow, (32, 2 * D)), 0.0).astype(bf16)
        grow = dot(grow, gain_comb(), NT)
        grow = jnp.where(p == 2, grow, 0.0).astype(bf16)
        low = jnp.concatenate([grow, jnp.zeros((32, D - 128), bf16)], axis=1)
        full = jnp.concatenate([g.astype(bf16), low], axis=0)
        sq[p] = dot(u512[...], full, TN).astype(bf16).reshape(BOX + (PAD, D))
        start(rs_q(p).core)

        @pl.when(p == 0)
        def _():
            rs_d[1].near_to_far()
            rs_u[1].near_to_far()
            rs_o.core_to_near()

        @pl.when(p == 1)
        def _():
            rs_d[1].end_far()
            start(ln_d)
            rs_u[1].end_far()
            start(ln_u[1])
            rs_o.near_to_far()
            rs_q(0).core_to_near()

        return gg1

    lax.fori_loop(0, PAIRS, backward_pair, jnp.zeros((D, 128), f32))

    def da_rows(i):
        rows = slice(512 * i, 512 * i + 512)
        da = jnp.zeros((512, D), f32)
        for p in range(PAIRS):
            w = jnp.concatenate([wqkv[:, j * D + p * 128:j * D + p * 128 + 128] for j in range(3)], axis=1)
            da = da + dot(dqkv[p, rows, :], w, NT)
        oacc[rows, :] = dh[rows, :] + norm_back(da * G1, xhat[rows, :], rstd[rows, 0:1])
        copy = pltpu.make_async_copy(oacc.at[rows], gx_hbm.at[rows], lsem.at[1 + i])
        copy.start()
        return copy

    def from_slot(v, width, rows, dst, first=0, cols=None):
        for k, j in enumerate(cols if cols is not None else range(first, first + v.shape[1] // 128)):
            dst[pl.ds(j, rows, stride=width), :] = v[0:rows, 128 * k:128 * k + 128]

    rs_q(0).near_to_far()
    rs_o.end_far()
    start(ln_o)
    rs_q(1).core_to_near()
    gx0 = da_rows(0)
    rs_q(2).core_to_near()
    rs_q(0).end_far()
    start(ln_q(0))
    rs_q(1).near_to_far()
    gx1 = da_rows(1)
    rs_q(2).near_to_far()
    rs_q(1).end_far()
    start(ln_q(1))
    for j in range(2):
        wait(ln_u[j])
        from_slot(line_sum(su.at[j], zu.at[j]), 12, 12, ou, 6 * j)
    wait(ln_d)
    from_slot(line_sum(sd, zd), 3, 48, od)
    wait(ln_o)
    from_slot(line_sum(so, zo), 3, 12, oo)
    rs_q(2).end_far()
    start(ln_q(2))
    for p in range(PAIRS):
        wait(ln_q(p))
        v = line_sum(sq.at[p], zq.at[p])
        from_slot(v, 9, 12, oq, cols=(p, 3 + p, 6 + p))
        if p == 2:
            og[...] = v[12:13, 0:24]
    out_copy.wait()
    gx0.wait()
    gx1.wait()


def vm(shape, dtype):
    return pltpu.VMEM(shape, dtype)


WIDE = ((PAIRS,), (PAD, D)), ((), (PAD, D)), ((2,), (PAD, HALF)), ((), (48, D))


def layer(x, seg, fq, fo, fu, fd, fg, dy):
    spec = pl.BlockSpec(memory_space=pltpu.VMEM)
    hbm = pl.BlockSpec(memory_space=pl.ANY)
    dma = pltpu.SemaphoreType.DMA
    scratch = [
        vm((PAIRS,) + BOX + (PAD, D), bf16), vm(BOX + (PAD, D), bf16), vm(BOX + (PAD, FF), bf16),
        vm(BOX + (48, D), bf16),
        vm((D + 32, 512), bf16), vm((D, 3 * D), bf16), vm((D, D), bf16), vm((D, FF), bf16), vm((FF, D), bf16),
        vm((8, D), f32), vm((144, 128), f32), vm((PAD, 128), f32),
        vm((T, D), f32), vm((T, 128), f32), vm((T, D), bf16), vm((PAIRS, T, 128), bf16), vm((PAIRS, T, 128), bf16),
        vm((PAIRS, TILES, 128, 256), bf16), vm((T, D), bf16), vm((D, T), bf16), vm((PAIRS, TILES, 8, 256), f32),
        vm((T, D), f32), vm((T, 128), f32), vm((T, D), bf16), vm((T, HALF), bf16), vm((T, HALF), bf16),
        vm((T, D), f32), vm((T, D), f32), vm((T, D), bf16), vm((T, D), f32), vm((T, D), bf16),
        vm((PAIRS, TILES, 128, 256), bf16), vm((PAIRS, T, 128), f32), vm((PAIRS, T, 128), f32),
        vm((PAIRS, T, D), bf16),
        [vm((PAIRS, ke - ks, 256), bf16) for ks, ke in KEYS],
        [vm((ke - ks, 128), f32) for ks, ke in KEYS],
    ]
    for lead in (BOX, BOX[:4], BOX[:2], BOX[:2], BOX[:1], BOX[:1], (3,)):
        scratch += [vm(g + lead + s, bf16) for g, s in WIDE]
    scratch += [dma((6, 2, 8)), dma((8, 2, 8)), dma((3,))]
    flops = 2 * T * (3 * (3 * D * D + D * D + 2 * D * FF)) + 12 * 2 * 330 * T * D
    return pl.pallas_call(
        layer_kernel,
        out_shape=[
            jax.ShapeDtypeStruct((T, D), bf16),
            jax.ShapeDtypeStruct((T, D), f32),
            jax.ShapeDtypeStruct(fq.shape, f32),
            jax.ShapeDtypeStruct(fo.shape, f32),
            jax.ShapeDtypeStruct(fu.shape, f32),
            jax.ShapeDtypeStruct(fd.shape, f32),
            jax.ShapeDtypeStruct(fg.shape, f32),
        ],
        in_specs=[spec] * 8,
        out_specs=[hbm] * 2 + [spec] * 5,
        scratch_shapes=scratch,
        compiler_params=pltpu.CompilerParams(collective_id=0, has_side_effects=True, vmem_limit_bytes=62 * 2**20),
        cost_estimate=pl.CostEstimate(flops=flops, bytes_accessed=5 * 2**20, transcendentals=T * (FF + 2508)),
        name="layer",
    )(x, seg, fq, fo, fu, fd, fg, dy)


def body_direct(tokens, seg_ids, w_qkv, w_out, w_up, w_down, norm_gains, cotangent):
    def lanes(w):
        return w.reshape(-1, 128)

    out, gx, oq, oo, ou, od, og = layer(
        tokens[0], seg_ids, lanes(w_qkv), lanes(w_out), lanes(w_up), lanes(w_down), norm_gains.reshape(1, -1),
        cotangent[0])
    return (out[None], gx[None], oq.reshape(-1), oo.reshape(-1), ou.reshape(-1), od.reshape(-1), og.reshape(-1))


def plain_kernel(x_ref, seg_ref, wqkv_ref, wo_ref, w1_ref, w2_ref, gain_ref, dy_ref,
           out_ref, gx_ref, gqkv_ref, gout_ref, gup_ref, gdown_ref, ggain_ref,
           xhat, rstd, a, k_p, v_p, qz, ctx, ctxt, h, rinv, b, act, du, dh, dhr, dz, dkacc, dvacc, dqkv, *rest):
    es, biases = rest[:8], rest[8:]
    G1 = gain_ref[0:1, :]
    G2 = gain_ref[1:2, :]
    R = 256
    qz[...] = jnp.zeros_like(qz)
    dz[...] = jnp.zeros_like(dz)

    def stage_a(i, _):
        rows = pl.ds(pl.multiple_of(i * R, R), R)
        n, r = norm_rows(x_ref[rows, :].astype(f32))
        xhat[rows, :] = n
        rstd[0, rows, :] = jnp.broadcast_to(r, (R, 128))
        al = (n * G1).astype(bf16)
        a[rows, :] = al
        q = dot(al, wqkv_ref[:, 0:D]).astype(bf16).astype(f32) * 0.125
        kk = dot(al, wqkv_ref[:, D:2 * D]).astype(bf16)
        vv = dot(al, wqkv_ref[:, 2 * D:]).astype(bf16)
        for p in range(PAIRS):
            k_p[p, rows, :] = kk[:, 128 * p:128 * p + 128]
            v_p[p, rows, :] = vv[:, 128 * p:128 * p + 128]
            for s in range(R // 128):
                qt = q[128 * s:128 * s + 128, 128 * p:128 * p + 128].T.astype(bf16)
                qz[p, i * (R // 128) + s, 0:64, 0:128] = qt[0:64]
                qz[p, i * (R // 128) + s, 64:128, 128:256] = qt[64:128]
        return 0

    lax.fori_loop(0, T // R, stage_a, 0)

    segf = seg_ref[0:1, :].astype(f32)
    segcol = jnp.broadcast_to(segf, (128, T)).T
    for t in range(8):
        ks, ke = KEYS[t]
        biases[t][...] = jnp.where(segcol[ks:ke, :] == segf[:, 128 * t:128 * t + 128], 0.0, NEG)

    def att(p, _):
        lanes = pl.ds(pl.multiple_of(p * 128, 128), 128)
        for t in range(8):
            ks, ke = KEYS[t]
            s = dot(k_p[p, ks:ke, :], qz[p, t])
            ee, ri = [], []
            for half in range(2):
                sh = s[:, 128 * half:128 * half + 128] + biases[t][...]
                m = jnp.max(sh, axis=0, keepdims=True)
                ex = jnp.exp(sh - m)
                ri.append(1.0 / jnp.sum(ex, axis=0, keepdims=True))
                ee.append(ex.astype(bf16))
            e = jnp.concatenate(ee, axis=1)
            es[t][p] = e
            rr = jnp.concatenate(ri, axis=1)
            rinv[p, t] = jnp.broadcast_to(rr, (8, 256))
            ct = dot(v_p[p, ks:ke, :], e, TN)
            ct = jnp.concatenate([ct[0:64, 0:128] * ri[0], ct[64:128, 128:256] * ri[1]], axis=0)
            ctxt[lanes, 128 * t:128 * t + 128] = ct.astype(bf16)
            ctx[128 * t:128 * t + 128, lanes] = ct.T.astype(bf16)
        return 0

    lax.fori_loop(0, PAIRS, att, 0)

    FC = 512
    def stage_d(i, gacc):
        rows = pl.ds(pl.multiple_of(i * R, R), R)
        hh = x_ref[rows, :].astype(f32) + dot(ctx[rows, :], wo_ref[...])
        n, r = norm_rows(hh)
        bl = (n * G2).astype(bf16)
        b[rows, :] = bl
        dyl = dy_ref[rows, :]
        o = hh
        db = jnp.zeros((R, D), f32)
        for c in range(FF // FC):
            cols = slice(c * FC, c * FC + FC)
            u = dot(bl, w1_ref[:, cols])
            phi = 0.5 * (1.0 + lax.erf(u * 0.7071067811865476))
            al = (u * phi).astype(bf16)
            act[rows, cols] = al
            o = o + dot(al, w2_ref[cols, :])
            gp = phi + u * jnp.exp(-0.5 * u * u) * 0.3989422804014327
            dul = (gp * dot(dyl, w2_ref[cols, :], NT)).astype(bf16)
            du[rows, cols] = dul
            db = db + dot(dul, w1_ref[:, cols], NT)
        out_ref[rows, :] = o.astype(bf16)
        gacc = gacc + jnp.sum(db * n, axis=0, keepdims=True)
        dhl = dyl.astype(f32) + norm_back(db * G2, n, r)
        dh[rows, :] = dhl
        dhrl = dhl.astype(bf16)
        dhr[rows, :] = dhrl
        dct = dot(wo_ref[...], dhrl, NT)
        for p in range(PAIRS):
            for s in range(R // 128):
                tt = i * (R // 128) + s
                ri = rinv[p, tt, 0:1, :]
                dz[p, tt, 0:64, 0:128] = (dct[128 * p:128 * p + 64, 128 * s:128 * s + 128].astype(bf16).astype(f32) * ri[:, 0:128]).astype(bf16)
                dz[p, tt, 64:128, 128:256] = (dct[128 * p + 64:128 * p + 128, 128 * s:128 * s + 128].astype(bf16).astype(f32) * ri[:, 128:256]).astype(bf16)
        return gacc

    def sd():
        ggain_ref[1:2, :] = lax.fori_loop(0, T // R, stage_d, jnp.zeros((1, D), f32))
    sd()

    def w_down(i, _):
        cols = pl.ds(pl.multiple_of(i * 256, 256), 256)
        gdown_ref[cols, :] = dot(act[:, cols], dy_ref[...], TN)
        gup_ref[:, cols] = dot(b[...], du[:, cols], TN)
        return 0

    lax.fori_loop(0, FF // 256, w_down, 0)
    gout_ref[...] = dot(ctxt[...], dhr[...])

    dkacc[...] = jnp.zeros_like(dkacc)
    dvacc[...] = jnp.zeros_like(dvacc)
    def attb(p, _):
        lanes = pl.ds(pl.multiple_of(p * 128, 128), 128)
        for t in range(8):
            ks, ke = KEYS[t]
            dzl = dz[p, t]
            dp = dot(v_p[p, ks:ke, :], dzl)
            e = es[t][p]
            ef = e.astype(f32)
            tt = ef * dp
            c = jnp.sum(tt, axis=0, keepdims=True) * rinv[p, t, 0:1, :]
            ds = (tt - ef * c).astype(bf16)
            dvacc[p, ks:ke, :] += dot(e, dzl, NT)
            dkacc[p, ks:ke, :] += dot(ds, qz[p, t], NT)
            dqt = dot(k_p[p, ks:ke, :], ds, TN)
            dqt = jnp.concatenate([dqt[0:64, 0:128], dqt[64:128, 128:256]], axis=0) * 0.125
            dqkv[128 * t:128 * t + 128, lanes] = dqt.T.astype(bf16)
        return 0

    lax.fori_loop(0, PAIRS, attb, 0)
    for p in range(PAIRS):
        dqkv[:, D + 128 * p:D + 128 * p + 128] = dkacc[p].astype(bf16)
        dqkv[:, 2 * D + 128 * p:2 * D + 128 * p + 128] = dvacc[p].astype(bf16)

    def w_qkv(i, _):
        cols = pl.ds(pl.multiple_of(i * 384, 384), 384)
        gqkv_ref[:, cols] = dot(a[...], dqkv[:, cols], TN)
        return 0

    lax.fori_loop(0, 3, w_qkv, 0)

    def stage_g(i, gacc):
        rows = pl.ds(pl.multiple_of(i * R, R), R)
        da = dot(dqkv[rows, :], wqkv_ref[...], NT)
        n = xhat[rows, :]
        gacc = gacc + jnp.sum(da * n, axis=0, keepdims=True)
        gx_ref[rows, :] = dh[rows, :] + norm_back(da * G1, n, rstd[0, rows, 0:1])
        return gacc

    def sg():
        ggain_ref[0:1, :] = lax.fori_loop(0, T // R, stage_g, jnp.zeros((1, D), f32))
    sg()


PLAIN_SCRATCH = [
    pltpu.VMEM((T, D), f32),
    pltpu.VMEM((1, T, 128), f32),
    pltpu.VMEM((T, D), bf16),
    pltpu.VMEM((PAIRS, T, 128), bf16),
    pltpu.VMEM((PAIRS, T, 128), bf16),
    pltpu.VMEM((PAIRS, 8, 128, 256), bf16),
    pltpu.VMEM((T, D), bf16),
    pltpu.VMEM((D, T), bf16),
    pltpu.VMEM((8, 128), f32),
    pltpu.VMEM((PAIRS, 8, 8, 256), f32),
    pltpu.VMEM((T, D), bf16),
    pltpu.VMEM((T, FF), bf16),
    pltpu.VMEM((T, FF), bf16),
    pltpu.VMEM((T, D), f32),
    pltpu.VMEM((T, D), bf16),
    pltpu.VMEM((PAIRS, 8, 128, 256), bf16),
    pltpu.VMEM((PAIRS, T, 128), f32),
    pltpu.VMEM((PAIRS, T, 128), f32),
    pltpu.VMEM((T, 3 * D), bf16),
] + [pltpu.VMEM((PAIRS, ke - ks, 256), bf16) for ks, ke in KEYS] + [pltpu.VMEM((ke - ks, 128), f32) for ks, ke in KEYS]


def plain_layer(x, seg, wqkv, wo, w1, w2, gains, dy):
    vm = pl.BlockSpec(memory_space=pltpu.VMEM)
    return pl.pallas_call(
        plain_kernel,
        out_shape=[
            jax.ShapeDtypeStruct((T, D), bf16),
            jax.ShapeDtypeStruct((T, D), f32),
            jax.ShapeDtypeStruct((D, 3 * D), f32),
            jax.ShapeDtypeStruct((D, D), f32),
            jax.ShapeDtypeStruct((D, FF), f32),
            jax.ShapeDtypeStruct((FF, D), f32),
            jax.ShapeDtypeStruct((2, D), f32),
        ],
        in_specs=[vm] * 8,
        out_specs=[vm] * 7,
        scratch_shapes=PLAIN_SCRATCH,
        compiler_params=pltpu.CompilerParams(vmem_limit_bytes=62 * 2**20),
        name="plain_layer",
    )(x, seg, wqkv, wo, w1, w2, gains, dy)


def body_plain(tokens, seg_ids, w_qkv, w_out, w_up, w_down, norm_gains, cotangent):
    whole = [lax.all_gather(w, "fsdp", axis=0, tiled=True) for w in (w_qkv, w_out, w_up, w_down, norm_gains)]
    out, gx, *grads = plain_layer(
        tokens[0], seg_ids, whole[0].reshape(D, 3 * D), whole[1].reshape(D, D), whole[2].reshape(D, FF),
        whole[3].reshape(FF, D), whole[4].astype(f32).reshape(2, D), cotangent[0])
    shards = [lax.psum_scatter(g.reshape(-1), "fsdp", scatter_dimension=0, tiled=True) for g in grads]
    return (out[None], gx[None], *shards)


def solution(mesh):
    direct = mesh.shape["fsdp"] == DEVICES
    rows, flat = P("fsdp", None, None), P("fsdp")
    return jax.shard_map(
        body_direct if direct else body_plain,
        mesh=mesh,
        in_specs=(rows, P("fsdp", None), flat, flat, flat, flat, flat, rows),
        out_specs=(rows, rows, flat, flat, flat, flat, flat),
        check_vma=False,
    )
```

time: 156 us -> 91.7 us (0.59)
  Pallas kernels: 141 us -> 84.5 us
  local copies, waits for them, and re-layouts: 12.8 us -> 6.4 us
    pallas_call x3 -> x1, Pallas kernels: 141 us -> 84.5 us  [layer(): pl.pallas_call(layer_kernel, out_shape=[jax.ShapeDtypeStruct((T, D), bf16...]
    reshape x9 -> x0, local copies, waits for them, and re-layouts: 9.69 us -> none  [the longest x1 1.53 us: body_direct(): ou[:12].reshape(-1)]
    unnamed x0 -> x19, local copies, waits for them, and re-layouts: none -> 6.4 us
    pad x3 -> x0, local copies, waits for them, and re-layouts: 1.9 us -> none  [the longest x2 1.24 us: pad_rows(): return jnp.pad(m, ((0, PAD - m.shape[0]), (0, 0)))]
where the time goes in v2:
time: 91.7 us; the launch traced here: 91.6 us
  Pallas kernels  84.5 us (92%)
  local copies, waits for them, and re-layouts  6.4 us (7%)
    pallas_call x1, Pallas kernels, layer(): pl.pallas_call(layer_kernel, out_shape=[jax.ShapeDtypeStruct((T, D), bf16...  84.5 us
    unnamed x19, local copies, waits for them, and re-layouts  6.4 us

profile of v2, /device:TPU:0, one launch (start us, length us, event | category | flops | bytes accessed | tf_op | source)
XLA Modules:
  0.0 91.6 jit_solution(1386430700847084241)
XLA Ops:
  0.6 84.5 %layer.1 = (bf16[1024,384]{1,0:T(8,128)(2,1)}, f32[1024,384]{1,0:T(8,128)}, f32[108,128]{1,0:T(8,128)}, f32[36,128]{1,0:T(8,128)}, f32[144,128]{1,0:T(8,128)}, /*index=5*/f32[144,128]{1,0:T(8,128)}, f32[1,24]{1,0:T(1,128)}) custom-call(bf16[1024,384]{1,0:T(8,128)(2,1)} %bitcast.20, s32[1,1024]{1,0:T(1,128)} %seg_ref.1, bf16[108,128]{1,0:T(8,128)(2,1)} %bitcast.24, ...), custom_call_target="tpu_custom_call" | custom-call | flops 13985906688 | bytes 5242880 | tf_op jit(solution)/shard_map/layer/pallas_call | solution.py:570
  85.1 0.0 copy-start
  85.1 2.2 %copy.22 = bf16[1,1024,384]{2,1,0:T(8,128)(2,1)} copy(bf16[1,1024,384]{2,1,0:T(8,128)(2,1)} %bitcast.15) | data formatting | bytes 1572864
  87.4 0.0 copy-done
  87.4 0.0 copy-start.3
  87.4 0.0 copy-start.4
  87.4 0.0 copy-start.2
  87.4 0.0 copy-start.1
  87.4 0.0 copy-start.5
  87.4 1.1 %copy.23 = f32[1,1024,384]{2,1,0:T(8,128)} copy(f32[1,1024,384]{2,1,0:T(8,128)S(1)} %bitcast.14) | data formatting | bytes 3145728
  88.5 0.0 copy-done.3
  88.5 0.6 copy.24
  89.2 0.0 copy-done.4
  89.2 0.6 copy.25
  89.8 0.0 copy-done.2
  89.8 0.6 copy.26
  90.4 0.0 copy-done.1
  90.4 0.6 copy.27
  91.1 0.0 copy-done.5
  91.1 0.5 copy.28
Async XLA Ops:
  85.1 2.2 %copy-start = (f32[1024,384]{1,0:T(8,128)S(1)}, f32[1024,384]{1,0:T(8,128)}, u32[]{:S(2)}) copy-start(f32[1024,384]{1,0:T(8,128)} %get-tuple-element.15) | copy-start | bytes 4718596
  87.4 1.2 %copy-start.3 = (f32[108,128]{1,0:T(8,128)S(1)}, f32[108,128]{1,0:T(8,128)}, u32[]{:S(2)}) copy-start(f32[108,128]{1,0:T(8,128)} %get-tuple-element.16) | copy-start | bytes 165892
  87.4 1.8 %copy-start.4 = (f32[36,128]{1,0:T(8,128)S(1)}, f32[36,128]{1,0:T(8,128)}, u32[]{:S(2)}) copy-start(f32[36,128]{1,0:T(8,128)} %get-tuple-element.17) | copy-start | bytes 55300
  87.4 2.4 %copy-start.2 = (f32[144,128]{1,0:T(8,128)S(1)}, f32[144,128]{1,0:T(8,128)}, u32[]{:S(2)}) copy-start(f32[144,128]{1,0:T(8,128)} %get-tuple-element.18) | copy-start | bytes 221188
  87.4 3.1 %copy-start.1 = (f32[144,128]{1,0:T(8,128)S(1)}, f32[144,128]{1,0:T(8,128)}, u32[]{:S(2)}) copy-start(f32[144,128]{1,0:T(8,128)} %get-tuple-element.19) | copy-start | bytes 221188
  87.4 3.7 %copy-start.5 = (f32[1,24]{1,0:T(1,128)S(1)}, f32[1,24]{1,0:T(1,128)}, u32[]{:S(2)}) copy-start(f32[1,24]{1,0:T(1,128)} %get-tuple-element.20) | copy-start | bytes 292

commit v3 on v2

--- a/solution.py
+++ b/solution.py
@@ -86,9 +86,6 @@
         self.make().wait()
 
 
-send = Copy
-
-
 def greet():
     z, y, x, c = place()
     barrier = pltpu.get_barrier_semaphore()
@@ -96,7 +93,7 @@
     partners += [(z ^ m, y, x, c) for m in (1, 2, 3)]
     for p in partners:
         pl.semaphore_signal(barrier, inc=1, device_id=device(*p), device_id_type=MESH)
-    pl.semaphore_wait(barrier, len(partners))
+    return lambda: pl.semaphore_wait(barrier, len(partners))
 
 
 def start(copies):
@@ -109,34 +106,41 @@
         q.wait()
 
 
-def gather_steps(b, sems, split):
+def line_of(b, sems):
     z, y, x, c = place()
-    zh, zl = z // 2, z % 2
-    own = b.at[zh, zl, y, x, c]
-    line = [send(own, own, sems, m - 1, (z ^ m, y, x, c)) for m in (1, 2, 3)]
+    own = b.at[z // 2, z % 2, y, x, c]
+    return [Copy(own, own, sems, m - 1, (z ^ m, y, x, c)) for m in (1, 2, 3)]
+
+
+def plane_direct(b, sems):
+    z, y, x, c = place()
     col = b.at[:, :, y, x, c]
-    near = [send(col, col, sems, 3, (z, y, 1 - x, c)), send(col, col, sems, 4, (z, 1 - y, x, c))]
-    core = [send(b.at[:, :, :, :, c], b.at[:, :, :, :, c], sems, 7, (z, y, x, 1 - c))]
-    if not split:
-        far = [send(col, col, sems, 5, (z, 1 - y, 1 - x, c))]
-        return [line, near + far, core]
-    fx, fy = b.at[:, 0, y, 1 - x, c], b.at[:, 1, 1 - y, x, c]
-    far = [send(fx, fx, sems, 5, (z, 1 - y, x, c)), send(fy, fy, sems, 6, (z, y, 1 - x, c))]
-    return [line, near, far, core]
+    near = [Copy(col, col, sems, 3, (z, y, 1 - x, c)), Copy(col, col, sems, 4, (z, 1 - y, x, c)),
+            Copy(col, col, sems, 5, (z, 1 - y, 1 - x, c))]
+    return [near, [Copy(b.at[:, :, :, :, c], b.at[:, :, :, :, c], sems, 7, (z, y, x, 1 - c))]]
+
+
+def plane_split(b, sems, h=pl.ds(0, 2)):
+    z, y, x, c = place()
+    col = b.at[h, :, y, x, c]
+    near = [Copy(col, col, sems, 3, (z, y, 1 - x, c)), Copy(col, col, sems, 4, (z, 1 - y, x, c))]
+    fx, fy = b.at[h, 0, y, 1 - x, c], b.at[h, 1, 1 - y, x, c]
+    far = [Copy(fx, fx, sems, 5, (z, 1 - y, x, c)), Copy(fy, fy, sems, 6, (z, y, 1 - x, c))]
+    return [near, far, [Copy(b.at[h, :, :, :, c], b.at[h, :, :, :, c], sems, 7, (z, y, x, 1 - c))]]
 
 
 class Scatter:
     def __init__(self, s, rc, rx, ry, sx, sy, sems, h=pl.ds(0, 2), nh=2):
         z, y, x, c = place()
         self.s, self.rc, self.rx, self.ry, self.sx, self.sy, self.h0, self.nh = s, rc, rx, ry, sx, sy, h.start, nh
-        self.core = [send(s.at[h, :, :, :, 1 - c], rc.at[h], sems, 0, (z, y, x, 1 - c))]
+        self.core = [Copy(s.at[h, :, :, :, 1 - c], rc.at[h], sems, 0, (z, y, x, 1 - c))]
         self.near = [
-            send(s.at[h, 0, :, 1 - x, c], rx.at[h], sems, 1, (z, y, 1 - x, c)),
-            send(s.at[h, 1, 1 - y, :, c], ry.at[h], sems, 2, (z, 1 - y, x, c)),
+            Copy(s.at[h, 0, :, 1 - x, c], rx.at[h], sems, 1, (z, y, 1 - x, c)),
+            Copy(s.at[h, 1, 1 - y, :, c], ry.at[h], sems, 2, (z, 1 - y, x, c)),
         ]
         self.far = [
-            send(s.at[h, 0, 1 - y, x, c], sy.at[h], sems, 3, (z, 1 - y, x, c)),
-            send(s.at[h, 1, y, 1 - x, c], sx.at[h], sems, 4, (z, y, 1 - x, c)),
+            Copy(s.at[h, 0, 1 - y, x, c], sy.at[h], sems, 3, (z, 1 - y, x, c)),
+            Copy(s.at[h, 1, y, 1 - x, c], sx.at[h], sems, 4, (z, y, 1 - x, c)),
         ]
 
     def add_core(self):
@@ -181,7 +185,7 @@
 
 def line_steps(s, rz, sems):
     z, y, x, c = place()
-    return [send(s.at[(z ^ m) // 2, (z ^ m) % 2, y, x, c], rz.at[m - 1], sems, m + 4, (z ^ m, y, x, c))
+    return [Copy(s.at[(z ^ m) // 2, (z ^ m) % 2, y, x, c], rz.at[m - 1], sems, m + 4, (z ^ m, y, x, c))
             for m in (1, 2, 3)]
 
 
@@ -194,7 +198,7 @@
     x_ref, seg_ref, fq, fo, fu, fd, fg, dy_ref,
     out_hbm, gx_hbm, oq, oo, ou, od, og,
     bq, bo, bu, bd, u512, wqkv, wo, w1, w2, gains, flat, sf,
-    xhat, rstd, a, k_p, v_p, qz, ctx, ctxt, rinv, hhat, rstd2, b, act, du, oacc, dbacc, out_v, dh, dhr, dz,
+    xhat, rstd, a, k_p, v_p, qz, ctx, ctxt, rinv, hhat, rstd2, b, act, du, hid, dbacc, out_v, dh, dhr, dz,
     dkacc, dvacc, dqkv, es, biases,
     sq, so, su, sd, cq, co, cu, cd, xq, xo, xu, xd, yq, yo, yu, yd, vq, vo, vu, vd, hq, ho, hu, hd, zq, zo, zu, zd,
     gsem, ssem, lsem,
@@ -202,66 +206,68 @@
     z, y, x, c = place()
     zh, zl = z // 2, z % 2
 
+    greeted = greet()
     sf[...] = jnp.zeros_like(sf)
 
     def to_slot(src, width, rows, dst, cols):
         n = rows * width
         flat[0:n, :] = src[...].astype(f32)
-        for j in range(width):
+        for j in cols:
+            piece = flat[pl.ds(j, rows, stride=width), :]
             if rows == 12:
-                sf[0:12, :] = flat[pl.ds(j, rows, stride=width), :]
+                sf[0:12, :] = piece
                 piece = sf[...]
-            else:
-                piece = flat[pl.ds(j, rows, stride=width), :]
-            dref, cj = dst(j) if callable(dst) else (dst, j)
-            dref[zh, zl, y, x, c, :, 128 * cj:128 * cj + 128] = piece.astype(bf16)
-
-    to_slot(fq, 9, 12, lambda j: (bq.at[j % 3], j // 3), None)
+            ref, k = dst(j)
+            ref[zh, zl, y, x, c, :, 128 * k:128 * k + 128] = piece.astype(bf16)
+            if width == 9 and j == 0:
+                sf[...] = jnp.zeros_like(sf)
+
     sf[12:13, 0:24] = fg[...].astype(f32)
-    sf[0:12, :] = flat[pl.ds(0, 12, stride=9), :]
-    bq[0, zh, zl, y, x, c, :, 0:128] = sf[...].astype(bf16)
-    sf[...] = jnp.zeros_like(sf)
-    greet()
-    gq = [gather_steps(bq.at[p], gsem.at[p], False) for p in range(PAIRS)]
+    to_slot(fq, 9, 12, lambda j: (bq.at[j % 3], j // 3), (0, 3, 6))
+    gq = [[line_of(bq.at[p], gsem.at[p])] + plane_direct(bq.at[p], gsem.at[p]) for p in range(PAIRS)]
+    go = [line_of(bo, gsem.at[3])] + plane_split(bo, gsem.at[3])
+    gu = [[line_of(bu.at[k], gsem.at[4 + k])] + plane_split(bu.at[k], gsem.at[4 + k]) for k in range(2)]
+    gd_line = line_of(bd, gsem.at[6])
+    gd = [plane_split(bd, gsem.at[6 + k], pl.ds(k, 1)) for k in range(2)]
+    greeted()
     start(gq[0][0])
+    to_slot(fq, 9, 12, lambda j: (bq.at[j % 3], j // 3), (1, 4, 7, 2, 5, 8))
     start(gq[1][0])
     start(gq[2][0])
-    to_slot(fo, 3, 12, bo, None)
-    to_slot(fu, 12, 12, bu, None)
-    to_slot(fd, 3, 48, bd, None)
-    go = gather_steps(bo, gsem.at[3], True)
-    gu = gather_steps(bu, gsem.at[4], True)
-    gd = gather_steps(bd, gsem.at[5], True)
-
+    to_slot(fo, 3, 12, lambda j: (bo, j), range(3))
+    start(go[0])
+    to_slot(fu, 12, 12, lambda j: (bu.at[j // 6], j % 6), range(12))
+    start(gu[0][0])
+    to_slot(fd, 3, 48, lambda j: (bd, j), range(3))
+    start(gd_line)
+    start(gu[1][0])
+
+    def norm_in(i, _):
+        rows = pl.ds(pl.multiple_of(i * 512, 512), 512)
+        n, r = norm_rows(x_ref[rows, :].astype(f32))
+        xhat[rows, :] = n
+        rstd[rows, :] = jnp.broadcast_to(r, (512, 128))
+        return 0
+
+    wait(gq[0][0])
+    start(gq[0][1])
+    lax.fori_loop(0, T // 512, norm_in, 0)
+    wait(gq[1][0])
+    start(gq[1][1])
+    wait(gq[2][0])
+    start(gq[2][1])
     u512[...] = spread_matrix(D + 32, 512)
     qz[...] = jnp.zeros_like(qz)
     dz[...] = jnp.zeros_like(dz)
-
-    def norm_in(i, _):
-        rows = pl.ds(pl.multiple_of(i * 256, 256), 256)
-        n, r = norm_rows(x_ref[rows, :].astype(f32))
-        xhat[rows, :] = n
-        rstd[rows, :] = jnp.broadcast_to(r, (256, 128))
-        return 0
-
-    lax.fori_loop(0, T // 256, norm_in, 0)
+    wait(gq[0][1])
+    start(gq[0][2])
+    wait(go[0])
+    start(go[1])
     segf = seg_ref[0:1, :].astype(f32)
     segcol = jnp.broadcast_to(segf, (128, T)).T
     for t in range(TILES):
         ks, ke = KEYS[t]
         biases[t][...] = jnp.where(segcol[ks:ke, :] == segf[:, 128 * t:128 * t + 128], 0.0, NEG)
-
-    wait(gq[0][0])
-    start(gq[0][1])
-    wait(gq[1][0])
-    start(gq[1][1])
-    wait(gq[2][0])
-    start(gq[2][1])
-    start(go[0])
-    start(gu[0])
-    start(gd[0])
-    wait(gq[0][1])
-    start(gq[0][2])
     wait(gq[0][2])
 
     wide = bq[0, ..., 0:128].reshape(512, 128)
@@ -273,12 +279,33 @@
     G2 = gains[1:2, :]
     a[...] = (xhat[...] * G1).astype(bf16)
 
+    def advance(*moves):
+        for g, k in moves:
+            wait(g[k])
+            start(g[k + 1])
+
+    def gather_progress(p, at):
+        steps = {
+            (0, 0): lambda: advance((gq[1], 1), (gu[0], 0)),
+            (0, 2): lambda: (advance((gq[2], 1), (go, 1)), wait(gd_line), start(gd[0][0])),
+            (1, 0): lambda: advance((gu[0], 1)),
+            (1, 2): lambda: (advance((gd[0], 0), (gu[1], 0)), start(gd[1][0])),
+            (2, 0): lambda: advance((go, 2)),
+            (2, 1): lambda: advance((gu[0], 2)),
+            (2, 2): lambda: advance((gd[0], 1)),
+        }
+        for q in range(PAIRS):
+            if (q, at) in steps:
+                @pl.when(p == q)
+                def _(q=q):
+                    steps[q, at]()
+
     def forward_pair(p, _):
         lanes = pl.ds(pl.multiple_of(p * 128, 128), 128)
 
         @pl.when(p > 0)
         def _():
-            wait(gather_steps(bq.at[p], gsem.at[p], False)[2])
+            wait(plane_direct(bq.at[p], gsem.at[p])[1])
 
         w = dot(u512[0:D, :], bq[p].reshape(512, D)).astype(bf16)
         for j in range(3):
@@ -294,38 +321,13 @@
                 qz[p, 4 * i + s, 0:64, 0:128] = qt[0:64]
                 qz[p, 4 * i + s, 64:128, 128:256] = qt[64:128]
 
-        @pl.when(p == 0)
-        def _():
-            wait(gq[1][1])
-            start(gq[1][2])
-            wait(gq[2][1])
-            start(gq[2][2])
-            wait(go[0])
-            start(go[1])
-            wait(gu[0])
-            start(gu[1])
-            wait(gd[0])
-            start(gd[1])
-
-        @pl.when(p == 1)
-        def _():
-            wait(go[1])
-            start(go[2])
-            wait(gu[1])
-            start(gu[2])
-
-        @pl.when(p == 2)
-        def _():
-            wait(gd[1])
-            start(gd[2])
-            wait(go[2])
-            start(go[3])
-            wait(gu[2])
-            start(gu[3])
-
-        for t in range(TILES):
+        gather_progress(p, 0)
+
+        def scores(t):
             ks, ke = KEYS[t]
-            s = dot(k_p[p, ks:ke, :], qz[p, t])
+            return dot(k_p[p, ks:ke, :], qz[p, t])
+
+        def weigh(t, s):
             ee, ri = [], []
             for half in range(2):
                 sh = s[:, 128 * half:128 * half + 128] + biases[t][...]
@@ -335,18 +337,31 @@
                 ee.append(ex.astype(bf16))
             e = jnp.concatenate(ee, axis=1)
             es[t][p] = e
-            rr = jnp.concatenate(ri, axis=1)
-            rinv[p, t] = jnp.broadcast_to(rr, (8, 256))
+            rinv[p, t] = jnp.broadcast_to(jnp.concatenate(ri, axis=1), (8, 256))
+            return t, e, ri
+
+        def mix(t, e, ri):
+            ks, ke = KEYS[t]
             ct = dot(v_p[p, ks:ke, :], e, TN)
             ct = jnp.concatenate([ct[0:64, 0:128] * ri[0], ct[64:128, 128:256] * ri[1]], axis=0)
             ctxt[lanes, 128 * t:128 * t + 128] = ct.astype(bf16)
             ctx[128 * t:128 * t + 128, lanes] = ct.T.astype(bf16)
+
+        s, last = scores(0), None
+        for t in range(TILES):
+            ahead = scores(t + 1) if t + 1 < TILES else None
+            now = weigh(t, s)
+            if last is not None:
+                mix(*last)
+            s, last = ahead, now
+            if t == 3:
+                gather_progress(p, 1)
+        mix(*last)
+        gather_progress(p, 2)
         return 0
 
     lax.fori_loop(0, PAIRS, forward_pair, 0)
 
-    wait(gd[2])
-    start(gd[3])
     wait(go[3])
     wo[...] = dot(u512[0:D, :], bo[...].reshape(512, D)).astype(bf16)
     for i in range(2):
@@ -356,11 +371,7 @@
         hhat[rows, :] = n
         rstd2[rows, :] = jnp.broadcast_to(r, (512, 128))
         b[rows, :] = (n * G2).astype(bf16)
-        oacc[rows, :] = hh
-    wait(gu[3])
-    w1[...] = dot(u512[0:D, :], bu[...].reshape(512, FF)).astype(bf16)
-    wait(gd[3])
-    w2[...] = bd[...].reshape(FF, D)
+        hid[rows, :] = hh
 
     rs_u = [Scatter(su.at[j], cu.at[j], xu.at[j], yu.at[j], vu.at[j], hu.at[j], ssem.at[j]) for j in range(2)]
     rs_d = [Scatter(sd, cd, xd, yd, vd, hd, ssem.at[2 + j], pl.ds(j, 1), 1) for j in range(2)]
@@ -371,13 +382,15 @@
 
     for j in range(2):
         cols = slice(HALF * j, HALF * j + HALF)
+        wait(gu[j][3])
+        w1[:, cols] = dot(u512[0:D, :], bu[j].reshape(512, HALF)).astype(bf16)
+        wait(gd[j][2])
+        w2[cols, :] = bd[j].reshape(HALF, D)
         for i in range(2):
             rows = slice(512 * i, 512 * i + 512)
             u = dot(b[rows, :], w1[:, cols])
             phi = 0.5 * (1.0 + lax.erf(u * 0.7071067811865476))
-            al = (u * phi).astype(bf16)
-            act[rows, :] = al
-            oacc[rows, :] += dot(al, w2[cols, :])
+            act[rows, cols] = (u * phi).astype(bf16)
             gp = phi + u * jnp.exp(-0.5 * u * u) * 0.3989422804014327
             dul = (gp * dot(dy_ref[rows, :], w2[cols, :], NT)).astype(bf16)
             du[rows, :] = dul
@@ -386,25 +399,19 @@
                 dbacc[rows, :] = db
             else:
                 dbacc[rows, :] += db
-            if j == 1:
-                if i == 0:
-                    rs_d[0].core_to_near()
-                    rs_u[0].core_to_near()
-                else:
-                    rs_d[0].near_to_far()
-                    rs_u[0].near_to_far()
-        sd[j] = dot(act[...], dy_ref[...], TN).astype(bf16).reshape((2, 2, 2, 2, 48, D))
+            if (j, i) == (0, 0):
+                advance((gu[1], 1), (gd[1], 0))
+            if (j, i) == (0, 1):
+                advance((gu[1], 2), (gd[1], 1))
+            if (j, i) == (1, 0):
+                rs_d[0].core_to_near()
+                rs_u[0].core_to_near()
+        sd[j] = dot(act[:, cols], dy_ref[...], TN).astype(bf16).reshape((2, 2, 2, 2, 48, D))
         start(rs_d[j].core)
         gup = dot(b[...], du[...], TN).astype(bf16)
         su[j] = dot(u512[0:D, :], gup, TN).astype(bf16).reshape(BOX + (PAD, HALF))
         start(rs_u[j].core)
 
-    out_v[...] = oacc[...].astype(bf16)
-    out_copy = pltpu.make_async_copy(out_v, out_hbm, lsem.at[0])
-    out_copy.start()
-    rs_d[0].end_far()
-    rs_u[0].end_far()
-    start(ln_u[0])
     gg2 = jnp.zeros((1, D), f32)
     for i in range(2):
         rows = slice(512 * i, 512 * i + 512)
@@ -424,11 +431,15 @@
                 low = dct[128 * p + 64:128 * p + 128, 128 * s:128 * s + 128].astype(bf16).astype(f32)
                 dz[p, t, 0:64, 0:128] = (top * ri[:, 0:128]).astype(bf16)
                 dz[p, t, 64:128, 128:256] = (low * ri[:, 128:256]).astype(bf16)
+        if i == 0:
+            rs_d[0].near_to_far()
+            rs_u[0].near_to_far()
+            rs_d[1].core_to_near()
+        else:
+            rs_u[1].core_to_near()
     gout = dot(ctxt[...], dhr[...]).astype(bf16)
     so[...] = dot(u512[0:D, :], gout, TN).astype(bf16).reshape(BOX + (PAD, D))
     start(rs_o.core)
-    rs_d[1].core_to_near()
-    rs_u[1].core_to_near()
 
     dkacc[...] = jnp.zeros_like(dkacc)
     dvacc[...] = jnp.zeros_like(dvacc)
@@ -439,22 +450,58 @@
     def ln_q(p):
         return line_steps(sq.at[p], zq.at[p], ssem.at[5 + p])
 
+    def scatter_progress(p, at):
+        def ends(*pairs):
+            for r, line in pairs:
+                r.end_far()
+                if line is not None:
+                    start(line)
+
+        steps = {
+            (0, 0): lambda: rs_o.core_to_near(),
+            (0, 1): lambda: ends((rs_d[0], None), (rs_u[0], ln_u[0])),
+            (1, 0): lambda: (rs_d[1].near_to_far(), rs_q(0).core_to_near()),
+            (1, 1): lambda: rs_u[1].near_to_far(),
+            (2, 0): lambda: (ends((rs_d[1], ln_d)), rs_o.near_to_far()),
+            (2, 1): lambda: (ends((rs_u[1], ln_u[1])), rs_q(0).near_to_far(), rs_q(1).core_to_near()),
+        }
+        for q in range(PAIRS):
+            if (q, at) in steps:
+                @pl.when(p == q)
+                def _(q=q):
+                    steps[q, at]()
+
     def backward_pair(p, gg1):
         lanes = pl.ds(pl.multiple_of(p * 128, 128), 128)
-        for t in range(TILES):
+        def pulls(t):
             ks, ke = KEYS[t]
-            dzl = dz[p, t]
-            dp = dot(v_p[p, ks:ke, :], dzl)
-            e = es[t][p]
-            ef = e.astype(f32)
-            tt = ef * dp
+            return dot(v_p[p, ks:ke, :], dz[p, t])
+
+        def weigh(t, dp):
+            e = es[t][p].astype(f32)
+            tt = e * dp
             cc = jnp.sum(tt, axis=0, keepdims=True) * rinv[p, t, 0:1, :]
-            ds = (tt - ef * cc).astype(bf16)
-            dvacc[p, ks:ke, :] += dot(e, dzl, NT)
+            return t, (tt - e * cc).astype(bf16)
+
+        def spread(t, ds):
+            ks, ke = KEYS[t]
+            dvacc[p, ks:ke, :] += dot(es[t][p], dz[p, t], NT)
             dkacc[p, ks:ke, :] += dot(ds, qz[p, t], NT)
             dqt = dot(k_p[p, ks:ke, :], ds, TN)
             dqt = jnp.concatenate([dqt[0:64, 0:128], dqt[64:128, 128:256]], axis=0) * 0.125
             dqkv[p, 128 * t:128 * t + 128, 0:128] = dqt.T.astype(bf16)
+
+        dp, last = pulls(0), None
+        for t in range(TILES):
+            ahead = pulls(t + 1) if t + 1 < TILES else None
+            now = weigh(t, dp)
+            if last is not None:
+                spread(*last)
+            dp, last = ahead, now
+            if t == 3:
+                scatter_progress(p, 0)
+        spread(*last)
+        scatter_progress(p, 1)
         dqkv[p, :, 128:256] = dkacc[p].astype(bf16)
         dqkv[p, :, 256:384] = dvacc[p].astype(bf16)
         g = dot(a[...], dqkv[p], TN)
@@ -471,21 +518,6 @@
         sq[p] = dot(u512[...], full, TN).astype(bf16).reshape(BOX + (PAD, D))
         start(rs_q(p).core)
 
-        @pl.when(p == 0)
-        def _():
-            rs_d[1].near_to_far()
-            rs_u[1].near_to_far()
-            rs_o.core_to_near()
-
-        @pl.when(p == 1)
-        def _():
-            rs_d[1].end_far()
-            start(ln_d)
-            rs_u[1].end_far()
-            start(ln_u[1])
-            rs_o.near_to_far()
-            rs_q(0).core_to_near()
-
         return gg1
 
     lax.fori_loop(0, PAIRS, backward_pair, jnp.zeros((D, 128), f32))
@@ -496,8 +528,8 @@
         for p in range(PAIRS):
             w = jnp.concatenate([wqkv[:, j * D + p * 128:j * D + p * 128 + 128] for j in range(3)], axis=1)
             da = da + dot(dqkv[p, rows, :], w, NT)
-        oacc[rows, :] = dh[rows, :] + norm_back(da * G1, xhat[rows, :], rstd[rows, 0:1])
-        copy = pltpu.make_async_copy(oacc.at[rows], gx_hbm.at[rows], lsem.at[1 + i])
+        dbacc[rows, :] = dh[rows, :] + norm_back(da * G1, xhat[rows, :], rstd[rows, 0:1])
+        copy = pltpu.make_async_copy(dbacc.at[rows], gx_hbm.at[rows], lsem.at[i])
         copy.start()
         return copy
 
@@ -505,19 +537,26 @@
         for k, j in enumerate(cols if cols is not None else range(first, first + v.shape[1] // 128)):
             dst[pl.ds(j, rows, stride=width), :] = v[0:rows, 128 * k:128 * k + 128]
 
-    rs_q(0).near_to_far()
+    def out_rows(i):
+        rows = slice(512 * i, 512 * i + 512)
+        out_v[rows, :] = (hid[rows, :] + dot(act[rows, :], w2[...])).astype(bf16)
+        copy = pltpu.make_async_copy(out_v.at[rows], out_hbm.at[rows], lsem.at[2 + i])
+        copy.start()
+        return copy
+
+    done = [da_rows(0)]
+    rs_q(2).core_to_near()
     rs_o.end_far()
     start(ln_o)
-    rs_q(1).core_to_near()
-    gx0 = da_rows(0)
-    rs_q(2).core_to_near()
     rs_q(0).end_far()
     start(ln_q(0))
+    done.append(da_rows(1))
     rs_q(1).near_to_far()
-    gx1 = da_rows(1)
+    done.append(out_rows(0))
     rs_q(2).near_to_far()
     rs_q(1).end_far()
     start(ln_q(1))
+    done.append(out_rows(1))
     for j in range(2):
         wait(ln_u[j])
         from_slot(line_sum(su.at[j], zu.at[j]), 12, 12, ou, 6 * j)
@@ -533,9 +572,8 @@
         from_slot(v, 9, 12, oq, cols=(p, 3 + p, 6 + p))
         if p == 2:
             og[...] = v[12:13, 0:24]
-    out_copy.wait()
-    gx0.wait()
-    gx1.wait()
+    for q in done:
+        q.wait()
 
 
 def vm(shape, dtype):
@@ -550,13 +588,13 @@
     hbm = pl.BlockSpec(memory_space=pl.ANY)
     dma = pltpu.SemaphoreType.DMA
     scratch = [
-        vm((PAIRS,) + BOX + (PAD, D), bf16), vm(BOX + (PAD, D), bf16), vm(BOX + (PAD, FF), bf16),
+        vm((PAIRS,) + BOX + (PAD, D), bf16), vm(BOX + (PAD, D), bf16), vm((2,) + BOX + (PAD, HALF), bf16),
         vm(BOX + (48, D), bf16),
         vm((D + 32, 512), bf16), vm((D, 3 * D), bf16), vm((D, D), bf16), vm((D, FF), bf16), vm((FF, D), bf16),
         vm((8, D), f32), vm((144, 128), f32), vm((PAD, 128), f32),
         vm((T, D), f32), vm((T, 128), f32), vm((T, D), bf16), vm((PAIRS, T, 128), bf16), vm((PAIRS, T, 128), bf16),
         vm((PAIRS, TILES, 128, 256), bf16), vm((T, D), bf16), vm((D, T), bf16), vm((PAIRS, TILES, 8, 256), f32),
-        vm((T, D), f32), vm((T, 128), f32), vm((T, D), bf16), vm((T, HALF), bf16), vm((T, HALF), bf16),
+        vm((T, D), f32), vm((T, 128), f32), vm((T, D), bf16), vm((T, FF), bf16), vm((T, HALF), bf16),
         vm((T, D), f32), vm((T, D), f32), vm((T, D), bf16), vm((T, D), f32), vm((T, D), bf16),
         vm((PAIRS, TILES, 128, 256), bf16), vm((PAIRS, T, 128), f32), vm((PAIRS, T, 128), f32),
         vm((PAIRS, T, D), bf16),
@@ -565,7 +603,7 @@
     ]
     for lead in (BOX, BOX[:4], BOX[:2], BOX[:2], BOX[:1], BOX[:1], (3,)):
         scratch += [vm(g + lead + s, bf16) for g, s in WIDE]
-    scratch += [dma((6, 2, 8)), dma((8, 2, 8)), dma((3,))]
+    scratch += [dma((8, 2, 8)), dma((8, 2, 8)), dma((4,))]
     flops = 2 * T * (3 * (3 * D * D + D * D + 2 * D * FF)) + 12 * 2 * 330 * T * D
     return pl.pallas_call(
         layer_kernel,
@@ -587,13 +625,47 @@
     )(x, seg, fq, fo, fu, fd, fg, dy)
 
 
+def hand_over_kernel(*refs):
+    ins, outs, stage, sem = refs[:7], refs[7:14], refs[14:21], refs[21]
+    loads, stores = [], []
+    for i, (src, mid, dst) in enumerate(zip(ins, stage, outs)):
+        parts = PARTS if src.shape[0] == T else 1
+        n = src.shape[0] // parts
+        for k in range(parts):
+            rows = pl.ds(n * k, n)
+            loads.append(pltpu.make_async_copy(src.at[rows], mid.at[rows], sem.at[0, i, k]))
+            stores.append(pltpu.make_async_copy(mid.at[rows], dst.at[rows], sem.at[1, i, k]))
+    for q in loads:
+        q.start()
+    for p, q in zip(loads, stores):
+        p.wait()
+        q.start()
+    for q in stores:
+        q.wait()
+
+
+PARTS = 4
+
+
+def hand_over(arrays):
+    hbm = pl.BlockSpec(memory_space=pl.ANY)
+    return pl.pallas_call(
+        hand_over_kernel,
+        out_shape=[jax.ShapeDtypeStruct(v.shape, v.dtype) for v in arrays],
+        in_specs=[hbm] * 7,
+        out_specs=[hbm] * 7,
+        scratch_shapes=[pltpu.VMEM(v.shape, v.dtype) for v in arrays] + [pltpu.SemaphoreType.DMA((2, 7, PARTS))],
+        name="hand_over",
+    )(*arrays)
+
+
 def body_direct(tokens, seg_ids, w_qkv, w_out, w_up, w_down, norm_gains, cotangent):
     def lanes(w):
         return w.reshape(-1, 128)
 
-    out, gx, oq, oo, ou, od, og = layer(
+    out, gx, oq, oo, ou, od, og = hand_over(layer(
         tokens[0], seg_ids, lanes(w_qkv), lanes(w_out), lanes(w_up), lanes(w_down), norm_gains.reshape(1, -1),
-        cotangent[0])
+        cotangent[0]))
     return (out[None], gx[None], oq.reshape(-1), oo.reshape(-1), ou.reshape(-1), od.reshape(-1), og.reshape(-1))
 
 

time: 91.7 us -> 77.7 us (0.85)
  Pallas kernels: 84.5 us -> 76.7 us
  local copies, waits for them, and re-layouts: 6.4 us -> 0 us
    pallas_call x1, Pallas kernels: 84.5 us -> 73.6 us  [layer(): pl.pallas_call(layer_kernel, out_shape=[jax.ShapeDtypeStruct((T, D), bf16...]
    unnamed x19 -> x0, local copies, waits for them, and re-layouts: 6.4 us -> none
    pallas_call x0 -> x1, Pallas kernels: none -> 3.05 us  [hand_over(): pl.pallas_call(hand_over_kernel, out_shape=[jax.ShapeDtypeStruct(v.shape,...]
where the time goes in v3:
time: 77.7 us; the launch traced here: 77.5 us
  Pallas kernels  76.7 us (99%)
  between operations  0.82 us (1%)
    pallas_call x1, Pallas kernels, layer(): pl.pallas_call(layer_kernel, out_shape=[jax.ShapeDtypeStruct((T, D), bf16...  73.6 us
    pallas_call x1, Pallas kernels, hand_over(): pl.pallas_call(hand_over_kernel, out_shape=[jax.ShapeDtypeStruct(v.shape,...  3.05 us

profile of v3, /device:TPU:0, one launch (start us, length us, event | category | flops | bytes accessed | tf_op | source)
XLA Modules:
  0.0 77.5 jit_solution(7671572283588083696)
XLA Ops:
  0.6 73.6 %layer.1 = (bf16[1024,384]{1,0:T(8,128)(2,1)}, f32[1024,384]{1,0:T(8,128)}, f32[108,128]{1,0:T(8,128)}, f32[36,128]{1,0:T(8,128)}, f32[144,128]{1,0:T(8,128)}, /*index=5*/f32[144,128]{1,0:T(8,128)}, f32[1,24]{1,0:T(1,128)}) custom-call(bf16[1024,384]{1,0:T(8,128)(2,1)} %bitcast.15, s32[1,1024]{1,0:T(1,128)} %seg_ref.1, bf16[108,128]{1,0:T(8,128)(2,1)} %bitcast.23, ...), custom_call_target="tpu_custom_call" | custom-call | flops 13985906688 | bytes 5242880 | tf_op jit(solution)/shard_map/layer/pallas_call | solution.py:608
  74.3 3.0 %hand_over.1 = (bf16[1024,384]{1,0:T(8,128)(2,1)}, f32[1024,384]{1,0:T(8,128)}, f32[108,128]{1,0:T(8,128)}, f32[36,128]{1,0:T(8,128)}, f32[144,128]{1,0:T(8,128)}, /*index=5*/f32[144,128]{1,0:T(8,128)}, f32[1,24]{1,0:T(1,128)}) custom-call(bf16[1024,384]{1,0:T(8,128)(2,1)} %get-tuple-element.21.refs_0_, f32[1024,384]{1,0:T(8,128)} %get-tuple-element.22.refs_1_, ...), custom_call_target="tpu_custom_call" | custom-call | tf_op jit(solution)/shard_map/hand_over/pallas_call | solution.py:652

commit v4 on v3

--- a/solution.py
+++ b/solution.py
@@ -20,6 +20,7 @@
 NT = (((1,), (1,)), ((), ()))
 TN = (((0,), (0,)), ((), ()))
 DEVICES = 32
+AHEAD = 4
 
 
 def dot(a, b, dims=NN):
@@ -118,6 +119,14 @@
     near = [Copy(col, col, sems, 3, (z, y, 1 - x, c)), Copy(col, col, sems, 4, (z, 1 - y, x, c)),
             Copy(col, col, sems, 5, (z, 1 - y, 1 - x, c))]
     return [near, [Copy(b.at[:, :, :, :, c], b.at[:, :, :, :, c], sems, 7, (z, y, x, 1 - c))]]
+
+
+def plane_first(b, sems):
+    z, y, x, c = place()
+    own, plane = b.at[z // 2, z % 2, y, x, c], b.at[z // 2, z % 2, :, :, c]
+    near = [Copy(own, own, sems, m - 1, (z, y ^ (m >> 1), x ^ (m & 1), c)) for m in (1, 2, 3)]
+    line = [Copy(plane, plane, sems, m + 2, (z ^ m, y, x, c)) for m in (1, 2, 3)]
+    return [near, line, [Copy(b.at[:, :, :, :, c], b.at[:, :, :, :, c], sems, 7, (z, y, x, 1 - c))]]
 
 
 def plane_split(b, sems, h=pl.ds(0, 2)):
@@ -183,6 +192,31 @@
         self.add_far()
 
 
+class PlaneScatter(Scatter):
+    def __init__(self, s, rc, rp, sems):
+        z, y, x, c = place()
+        self.s, self.rc, self.rp, self.h0, self.nh = s, rc, rp, 0, 2
+        self.core = [Copy(s.at[:, :, :, :, 1 - c], rc, sems, 0, (z, y, x, 1 - c))]
+        self.plane = [
+            Copy(s.at[:, :, y ^ (m >> 1), x ^ (m & 1), c], rp.at[m - 1], sems, m, (z, y ^ (m >> 1), x ^ (m & 1), c))
+            for m in (1, 2, 3)]
+
+    def core_to_plane(self):
+        wait(self.core)
+        self.add_core()
+        start(self.plane)
+
+    def end_plane(self):
+        z, y, x, c = place()
+        wait(self.plane)
+        for i in range(2):
+            for j in range(2):
+                t = self.s[i, j, y, x, c].astype(f32)
+                for m in range(3):
+                    t = t + self.rp[m, i, j].astype(f32)
+                self.s[i, j, y, x, c] = t.astype(bf16)
+
+
 def line_steps(s, rz, sems):
     z, y, x, c = place()
     return [Copy(s.at[(z ^ m) // 2, (z ^ m) % 2, y, x, c], rz.at[m - 1], sems, m + 4, (z ^ m, y, x, c))
@@ -195,18 +229,24 @@
 
 
 def layer_kernel(
-    x_ref, seg_ref, fq, fo, fu, fd, fg, dy_ref,
+    x_hbm, seg_ref, fq, fo, fu, fd, fg, dy_hbm,
     out_hbm, gx_hbm, oq, oo, ou, od, og,
-    bq, bo, bu, bd, u512, wqkv, wo, w1, w2, gains, flat, sf,
-    xhat, rstd, a, k_p, v_p, qz, ctx, ctxt, rinv, hhat, rstd2, b, act, du, hid, dbacc, out_v, dh, dhr, dz,
+    bq, bo, bu, bd, u512, wqkv, wo, w1, gains, flat, sf,
+    xhat, rstd, a, k_p, v_p, qz, ctx, ctxt, rinv, hhat, rstd2, act, du, hid, dbacc, dh, dhr, dz,
     dkacc, dvacc, dqkv, es, biases,
-    sq, so, su, sd, cq, co, cu, cd, xq, xo, xu, xd, yq, yo, yu, yd, vq, vo, vu, vd, hq, ho, hu, hd, zq, zo, zu, zd,
-    gsem, ssem, lsem,
+    sd, cq, co, cu, cd, xq, xo, xu, xd, yu, yd, vu, vd, hu, hd, zq, zo, zu, zd,
+    x_ref, dy_ref, gsem, ssem, lsem,
 ):
     z, y, x, c = place()
     zh, zl = z // 2, z % 2
 
     greeted = greet()
+    b = out_v = ctx
+    sq, so, su = bq, bo, bu
+    get_x = pltpu.make_async_copy(x_hbm, x_ref, lsem.at[4])
+    get_x.start()
+    get_dy = pltpu.make_async_copy(dy_hbm, dy_ref, lsem.at[5])
+    get_dy.start()
     sf[...] = jnp.zeros_like(sf)
 
     def to_slot(src, width, rows, dst, cols):
@@ -226,7 +266,7 @@
     to_slot(fq, 9, 12, lambda j: (bq.at[j % 3], j // 3), (0, 3, 6))
     gq = [[line_of(bq.at[p], gsem.at[p])] + plane_direct(bq.at[p], gsem.at[p]) for p in range(PAIRS)]
     go = [line_of(bo, gsem.at[3])] + plane_split(bo, gsem.at[3])
-    gu = [[line_of(bu.at[k], gsem.at[4 + k])] + plane_split(bu.at[k], gsem.at[4 + k]) for k in range(2)]
+    gu = [[line_of(bu.at[0], gsem.at[4])] + plane_split(bu.at[0], gsem.at[4]), plane_first(bu.at[1], gsem.at[5])]
     gd_line = line_of(bd, gsem.at[6])
     gd = [plane_split(bd, gsem.at[6 + k], pl.ds(k, 1)) for k in range(2)]
     greeted()
@@ -251,6 +291,7 @@
 
     wait(gq[0][0])
     start(gq[0][1])
+    get_x.wait()
     lax.fori_loop(0, T // 512, norm_in, 0)
     wait(gq[1][0])
     start(gq[1][1])
@@ -261,6 +302,8 @@
     dz[...] = jnp.zeros_like(dz)
     wait(gq[0][1])
     start(gq[0][2])
+    wait(gu[1][0])
+    start(gu[1][1])
     wait(go[0])
     start(go[1])
     segf = seg_ref[0:1, :].astype(f32)
@@ -268,11 +311,12 @@
     for t in range(TILES):
         ks, ke = KEYS[t]
         biases[t][...] = jnp.where(segcol[ks:ke, :] == segf[:, 128 * t:128 * t + 128], 0.0, NEG)
+    comb, mask = gain_comb(), gain_mask()
     wait(gq[0][2])
 
     wide = bq[0, ..., 0:128].reshape(512, 128)
     g32 = dot(u512[D:, :], wide).astype(bf16)
-    gall = jnp.sum(jnp.where(gain_mask(), dot(g32, gain_comb()), 0.0), axis=0, keepdims=True)
+    gall = jnp.sum(jnp.where(mask, dot(g32, comb), 0.0), axis=0, keepdims=True)
     gains[0:1, :] = gall[:, 0:D]
     gains[1:2, :] = gall[:, D:]
     G1 = gains[0:1, :]
@@ -284,32 +328,12 @@
             wait(g[k])
             start(g[k + 1])
 
-    def gather_progress(p, at):
-        steps = {
-            (0, 0): lambda: advance((gq[1], 1), (gu[0], 0)),
-            (0, 2): lambda: (advance((gq[2], 1), (go, 1)), wait(gd_line), start(gd[0][0])),
-            (1, 0): lambda: advance((gu[0], 1)),
-            (1, 2): lambda: (advance((gd[0], 0), (gu[1], 0)), start(gd[1][0])),
-            (2, 0): lambda: advance((go, 2)),
-            (2, 1): lambda: advance((gu[0], 2)),
-            (2, 2): lambda: advance((gd[0], 1)),
-        }
-        for q in range(PAIRS):
-            if (q, at) in steps:
-                @pl.when(p == q)
-                def _(q=q):
-                    steps[q, at]()
-
-    def forward_pair(p, _):
-        lanes = pl.ds(pl.multiple_of(p * 128, 128), 128)
-
-        @pl.when(p > 0)
-        def _():
-            wait(plane_direct(bq.at[p], gsem.at[p])[1])
-
+    def project(p):
+        if p > 0:
+            wait(gq[p][2])
         w = dot(u512[0:D, :], bq[p].reshape(512, D)).astype(bf16)
         for j in range(3):
-            wqkv[:, pl.ds(pl.multiple_of(j * D + p * 128, 128), 128)] = w[:, 128 * j:128 * j + 128]
+            wqkv[:, j * D + p * 128:j * D + p * 128 + 128] = w[:, 128 * j:128 * j + 128]
         for i in range(2):
             rows = slice(512 * i, 512 * i + 512)
             qkv = dot(a[rows, :], w)
@@ -321,47 +345,60 @@
                 qz[p, 4 * i + s, 0:64, 0:128] = qt[0:64]
                 qz[p, 4 * i + s, 64:128, 128:256] = qt[64:128]
 
-        gather_progress(p, 0)
-
-        def scores(t):
-            ks, ke = KEYS[t]
-            return dot(k_p[p, ks:ke, :], qz[p, t])
-
-        def weigh(t, s):
-            ee, ri = [], []
-            for half in range(2):
-                sh = s[:, 128 * half:128 * half + 128] + biases[t][...]
-                m = jnp.max(sh, axis=0, keepdims=True)
-                ex = jnp.exp(sh - m)
-                ri.append(1.0 / jnp.sum(ex, axis=0, keepdims=True))
-                ee.append(ex.astype(bf16))
-            e = jnp.concatenate(ee, axis=1)
-            es[t][p] = e
-            rinv[p, t] = jnp.broadcast_to(jnp.concatenate(ri, axis=1), (8, 256))
-            return t, e, ri
-
-        def mix(t, e, ri):
-            ks, ke = KEYS[t]
-            ct = dot(v_p[p, ks:ke, :], e, TN)
-            ct = jnp.concatenate([ct[0:64, 0:128] * ri[0], ct[64:128, 128:256] * ri[1]], axis=0)
-            ctxt[lanes, 128 * t:128 * t + 128] = ct.astype(bf16)
-            ctx[128 * t:128 * t + 128, lanes] = ct.T.astype(bf16)
-
-        s, last = scores(0), None
-        for t in range(TILES):
-            ahead = scores(t + 1) if t + 1 < TILES else None
-            now = weigh(t, s)
-            if last is not None:
-                mix(*last)
-            s, last = ahead, now
-            if t == 3:
-                gather_progress(p, 1)
-        mix(*last)
-        gather_progress(p, 2)
-        return 0
-
-    lax.fori_loop(0, PAIRS, forward_pair, 0)
-
+    def scores(p, t):
+        ks, ke = KEYS[t]
+        return dot(k_p[p, ks:ke, :], qz[p, t])
+
+    def weigh(p, t, s):
+        ee, ri = [], []
+        for half in range(2):
+            sh = s[:, 128 * half:128 * half + 128] + biases[t][...]
+            m = jnp.max(sh, axis=0, keepdims=True)
+            ex = jnp.exp(sh - m)
+            ri.append(1.0 / jnp.sum(ex, axis=0, keepdims=True))
+            ee.append(ex.astype(bf16))
+        e = jnp.concatenate(ee, axis=1)
+        es[t][p] = e
+        rinv[p, t] = jnp.broadcast_to(jnp.concatenate(ri, axis=1), (8, 256))
+        return p, t, e, ri
+
+    def mix(p, t, e, ri):
+        ks, ke = KEYS[t]
+        ct = dot(v_p[p, ks:ke, :], e, TN)
+        ct = jnp.concatenate([ct[0:64, 0:128] * ri[0], ct[64:128, 128:256] * ri[1]], axis=0)
+        ctxt[128 * p:128 * p + 128, 128 * t:128 * t + 128] = ct.astype(bf16)
+        ctx[128 * t:128 * t + 128, 128 * p:128 * p + 128] = ct.T.astype(bf16)
+
+    def advance(*moves):
+        for g, k in moves:
+            wait(g[k])
+            start(g[k + 1])
+
+    moves = {
+        (0, 0): lambda: advance((gq[1], 1), (gu[0], 0)),
+        (0, 6): lambda: (advance((gq[2], 1), (go, 1)), wait(gd_line), start(gd[0][0])),
+        (1, 0): lambda: advance((gu[0], 1)),
+        (1, 6): lambda: (advance((gd[0], 0)), start(gd[1][0])),
+        (2, 0): lambda: advance((go, 2)),
+        (2, 4): lambda: advance((gu[0], 2)),
+        (2, 7): lambda: advance((gd[0], 1)),
+    }
+    project(0)
+    s, last = scores(0, 0), None
+    for n in range(PAIRS * TILES):
+        p, t = n // TILES, n % TILES
+        if (p, t) in moves:
+            moves[p, t]()
+        if t == AHEAD and p + 1 < PAIRS:
+            project(p + 1)
+        ahead = scores((n + 1) // TILES, (n + 1) % TILES) if n + 1 < PAIRS * TILES else None
+        now = weigh(p, t, s)
+        if last is not None:
+            mix(*last)
+        s, last = ahead, now
+    mix(*last)
+
+    get_dy.wait()
     wait(go[3])
     wo[...] = dot(u512[0:D, :], bo[...].reshape(512, D)).astype(bf16)
     for i in range(2):
@@ -375,42 +412,75 @@
 
     rs_u = [Scatter(su.at[j], cu.at[j], xu.at[j], yu.at[j], vu.at[j], hu.at[j], ssem.at[j]) for j in range(2)]
     rs_d = [Scatter(sd, cd, xd, yd, vd, hd, ssem.at[2 + j], pl.ds(j, 1), 1) for j in range(2)]
-    rs_o = Scatter(so, co, xo, yo, vo, ho, ssem.at[4])
+    rs_o = PlaneScatter(so, co, xo, ssem.at[4])
     ln_u = [line_steps(su.at[j], zu.at[j], ssem.at[j]) for j in range(2)]
     ln_d = line_steps(sd, zd, ssem.at[2])
     ln_o = line_steps(so, zo, ssem.at[4])
 
-    for j in range(2):
-        cols = slice(HALF * j, HALF * j + HALF)
-        wait(gu[j][3])
-        w1[:, cols] = dot(u512[0:D, :], bu[j].reshape(512, HALF)).astype(bf16)
-        wait(gd[j][2])
-        w2[cols, :] = bd[j].reshape(HALF, D)
-        for i in range(2):
-            rows = slice(512 * i, 512 * i + 512)
-            u = dot(b[rows, :], w1[:, cols])
-            phi = 0.5 * (1.0 + lax.erf(u * 0.7071067811865476))
-            act[rows, cols] = (u * phi).astype(bf16)
-            gp = phi + u * jnp.exp(-0.5 * u * u) * 0.3989422804014327
-            dul = (gp * dot(dy_ref[rows, :], w2[cols, :], NT)).astype(bf16)
-            du[rows, :] = dul
-            db = dot(dul, w1[:, cols], NT)
-            if j == 0:
-                dbacc[rows, :] = db
-            else:
-                dbacc[rows, :] += db
-            if (j, i) == (0, 0):
-                advance((gu[1], 1), (gd[1], 0))
-            if (j, i) == (0, 1):
-                advance((gu[1], 2), (gd[1], 1))
-            if (j, i) == (1, 0):
-                rs_d[0].core_to_near()
-                rs_u[0].core_to_near()
-        sd[j] = dot(act[:, cols], dy_ref[...], TN).astype(bf16).reshape((2, 2, 2, 2, 48, D))
+    def half(j):
+        return slice(HALF * j, HALF * j + HALF)
+
+    def block(i):
+        return slice(512 * i, 512 * i + 512)
+
+    def up(j, i):
+        return dot(b[block(i), :], w1[:, half(j)])
+
+    def bend(j, i, u):
+        phi = 0.5 * (1.0 + lax.erf(u * 0.7071067811865476))
+        act[block(i), half(j)] = (u * phi).astype(bf16)
+        return phi + u * jnp.exp(-0.5 * u * u) * 0.3989422804014327
+
+    def pull(j, i):
+        return dot(dy_ref[block(i), :], bd[j].reshape(HALF, D), NT)
+
+    def back(j, i, dul):
+        du[block(i), :] = dul
+        db = dot(dul, w1[:, half(j)], NT)
+        if j == 0:
+            dbacc[block(i), :] = db
+        else:
+            dbacc[block(i), :] += db
+
+    def down_gradient(j):
+        sd[j] = dot(act[:, half(j)], dy_ref[...], TN).astype(bf16).reshape((2, 2, 2, 2, 48, D))
         start(rs_d[j].core)
+
+    def up_gradient(j):
         gup = dot(b[...], du[...], TN).astype(bf16)
         su[j] = dot(u512[0:D, :], gup, TN).astype(bf16).reshape(BOX + (PAD, HALF))
         start(rs_u[j].core)
+
+    def arrive(j):
+        wait(gu[j][-1])
+        w1[:, half(j)] = dot(u512[0:D, :], bu[j].reshape(512, HALF)).astype(bf16)
+
+    arrive(0)
+    u, v = up(0, 0), up(0, 1)
+    gp0 = bend(0, 0, u)
+    du[block(0), :] = gp0.astype(bf16)
+    gp1 = bend(0, 1, v)
+    du[block(1), :] = gp1.astype(bf16)
+    advance((gd[1], 0), (gu[1], 1))
+    down_gradient(0)
+    wait(gd[0][2])
+    for i in range(2):
+        back(0, i, (du[block(i), :].astype(f32) * pull(0, i)).astype(bf16))
+    advance((gd[1], 1))
+    up_gradient(0)
+    arrive(1)
+    u, v = up(1, 0), up(1, 1)
+    gp0 = bend(1, 0, u)
+    du[block(0), :] = gp0.astype(bf16)
+    rs_d[0].core_to_near()
+    gp1 = bend(1, 1, v)
+    du[block(1), :] = gp1.astype(bf16)
+    down_gradient(1)
+    rs_u[0].core_to_near()
+    wait(gd[1][2])
+    for i in range(2):
+        back(1, i, (du[block(i), :].astype(f32) * pull(1, i)).astype(bf16))
+    up_gradient(1)
 
     gg2 = jnp.zeros((1, D), f32)
     for i in range(2):
@@ -441,87 +511,87 @@
     so[...] = dot(u512[0:D, :], gout, TN).astype(bf16).reshape(BOX + (PAD, D))
     start(rs_o.core)
 
-    dkacc[...] = jnp.zeros_like(dkacc)
-    dvacc[...] = jnp.zeros_like(dvacc)
-
-    def rs_q(p):
-        return Scatter(sq.at[p], cq.at[p], xq.at[p], yq.at[p], vq.at[p], hq.at[p], ssem.at[5 + p])
-
-    def ln_q(p):
-        return line_steps(sq.at[p], zq.at[p], ssem.at[5 + p])
-
-    def scatter_progress(p, at):
-        def ends(*pairs):
-            for r, line in pairs:
-                r.end_far()
-                if line is not None:
-                    start(line)
-
-        steps = {
-            (0, 0): lambda: rs_o.core_to_near(),
-            (0, 1): lambda: ends((rs_d[0], None), (rs_u[0], ln_u[0])),
-            (1, 0): lambda: (rs_d[1].near_to_far(), rs_q(0).core_to_near()),
-            (1, 1): lambda: rs_u[1].near_to_far(),
-            (2, 0): lambda: (ends((rs_d[1], ln_d)), rs_o.near_to_far()),
-            (2, 1): lambda: (ends((rs_u[1], ln_u[1])), rs_q(0).near_to_far(), rs_q(1).core_to_near()),
-        }
-        for q in range(PAIRS):
-            if (q, at) in steps:
-                @pl.when(p == q)
-                def _(q=q):
-                    steps[q, at]()
-
-    def backward_pair(p, gg1):
-        lanes = pl.ds(pl.multiple_of(p * 128, 128), 128)
-        def pulls(t):
-            ks, ke = KEYS[t]
-            return dot(v_p[p, ks:ke, :], dz[p, t])
-
-        def weigh(t, dp):
-            e = es[t][p].astype(f32)
-            tt = e * dp
-            cc = jnp.sum(tt, axis=0, keepdims=True) * rinv[p, t, 0:1, :]
-            return t, (tt - e * cc).astype(bf16)
-
-        def spread(t, ds):
-            ks, ke = KEYS[t]
-            dvacc[p, ks:ke, :] += dot(es[t][p], dz[p, t], NT)
-            dkacc[p, ks:ke, :] += dot(ds, qz[p, t], NT)
-            dqt = dot(k_p[p, ks:ke, :], ds, TN)
-            dqt = jnp.concatenate([dqt[0:64, 0:128], dqt[64:128, 128:256]], axis=0) * 0.125
-            dqkv[p, 128 * t:128 * t + 128, 0:128] = dqt.T.astype(bf16)
-
-        dp, last = pulls(0), None
-        for t in range(TILES):
-            ahead = pulls(t + 1) if t + 1 < TILES else None
-            now = weigh(t, dp)
-            if last is not None:
-                spread(*last)
-            dp, last = ahead, now
-            if t == 3:
-                scatter_progress(p, 0)
-        spread(*last)
-        scatter_progress(p, 1)
-        dqkv[p, :, 128:256] = dkacc[p].astype(bf16)
-        dqkv[p, :, 256:384] = dvacc[p].astype(bf16)
+
+    rs_q = [PlaneScatter(sq.at[p], cq.at[p], xq.at[p], ssem.at[5 + p]) for p in range(PAIRS)]
+    ln_q = [line_steps(sq.at[p], zq.at[p], ssem.at[5 + p]) for p in range(PAIRS)]
+
+    def ends(r, line=None):
+        r.end_far()
+        if line is not None:
+            start(line)
+
+    def plane_ends(r, line):
+        r.end_plane()
+        start(line)
+
+    def pulls(p, t):
+        ks, ke = KEYS[t]
+        return dot(v_p[p, ks:ke, :], dz[p, t])
+
+    def slope(p, t, dp):
+        e = es[t][p].astype(f32)
+        tt = e * dp
+        cc = jnp.sum(tt, axis=0, keepdims=True) * rinv[p, t, 0:1, :]
+        return p, t, (tt - e * cc).astype(bf16)
+
+    def spread(p, t, ds):
+        ks, ke = KEYS[t]
+        dv = dot(es[t][p], dz[p, t], NT)
+        dk = dot(ds, qz[p, t], NT)
+        if t == 0:
+            dvacc[p % 2] = jnp.zeros((T, 128), f32)
+            dkacc[p % 2] = jnp.zeros((T, 128), f32)
+        dvacc[p % 2, ks:ke, :] += dv
+        dkacc[p % 2, ks:ke, :] += dk
+        dqt = dot(k_p[p, ks:ke, :], ds, TN)
+        dqt = jnp.concatenate([dqt[0:64, 0:128], dqt[64:128, 128:256]], axis=0) * 0.125
+        dqkv[p, 128 * t:128 * t + 128, 0:128] = dqt.T.astype(bf16)
+
+    def pair_gradient(p, gg1):
+        dqkv[p, :, 128:256] = dkacc[p % 2].astype(bf16)
+        dqkv[p, :, 256:384] = dvacc[p % 2].astype(bf16)
         g = dot(a[...], dqkv[p], TN)
         for j in range(3):
-            wj = wqkv[:, pl.ds(pl.multiple_of(j * D + p * 128, 128), 128)].astype(f32)
-            gg1 = gg1 + wj * g[:, 128 * j:128 * j + 128]
-        gsum = jnp.sum(gg1.T, axis=0, keepdims=True) / G1
-        grow = jnp.concatenate([gsum, gg2], axis=1)
-        grow = jnp.where(gain_mask(), jnp.broadcast_to(grow, (32, 2 * D)), 0.0).astype(bf16)
-        grow = dot(grow, gain_comb(), NT)
-        grow = jnp.where(p == 2, grow, 0.0).astype(bf16)
-        low = jnp.concatenate([grow, jnp.zeros((32, D - 128), bf16)], axis=1)
-        full = jnp.concatenate([g.astype(bf16), low], axis=0)
-        sq[p] = dot(u512[...], full, TN).astype(bf16).reshape(BOX + (PAD, D))
-        start(rs_q(p).core)
-
+            gg1 = gg1 + wqkv[:, j * D + p * 128:j * D + p * 128 + 128].astype(f32) * g[:, 128 * j:128 * j + 128]
+        full = g.astype(bf16)
+        if p == PAIRS - 1:
+            gsum = jnp.sum(gg1.T, axis=0, keepdims=True) / G1
+            grow = jnp.concatenate([gsum, gg2], axis=1)
+            grow = jnp.where(gain_mask(), jnp.broadcast_to(grow, (32, 2 * D)), 0.0).astype(bf16)
+            grow = dot(grow, gain_comb(), NT).astype(bf16)
+            low = jnp.concatenate([grow, jnp.zeros((32, D - 128), bf16)], axis=1)
+            full = dot(u512[...], jnp.concatenate([full, low], axis=0), TN)
+        else:
+            full = dot(u512[0:D, :], full, TN)
+        sq[p] = full.astype(bf16).reshape(BOX + (PAD, D))
+        start(rs_q[p].core)
         return gg1
 
-    lax.fori_loop(0, PAIRS, backward_pair, jnp.zeros((D, 128), f32))
-
+    moves = {
+        (0, 4): lambda: rs_o.core_to_plane(),
+        (0, 6): lambda: (ends(rs_d[0]), ends(rs_u[0], ln_u[0])),
+        (1, 4): lambda: rs_q[0].core_to_plane(),
+        (1, 7): lambda: rs_d[1].near_to_far(),
+        (2, 0): lambda: rs_u[1].near_to_far(),
+        (2, 2): lambda: plane_ends(rs_o, ln_o),
+        (2, 4): lambda: (rs_q[1].core_to_plane(), plane_ends(rs_q[0], ln_q[0])),
+        (2, 6): lambda: (ends(rs_d[1], ln_d), ends(rs_u[1], ln_u[1])),
+    }
+    gg1 = jnp.zeros((D, 128), f32)
+    dp, last = pulls(0, 0), None
+    for n in range(PAIRS * TILES):
+        p, t = n // TILES, n % TILES
+        if (p, t) in moves:
+            moves[p, t]()
+        ahead = pulls((n + 1) // TILES, (n + 1) % TILES) if n + 1 < PAIRS * TILES else None
+        now = slope(p, t, dp)
+        if last is not None:
+            spread(*last)
+        dp, last = ahead, now
+        if t == 1 and p > 0:
+            gg1 = pair_gradient(p - 1, gg1)
+    spread(*last)
+    pair_gradient(PAIRS - 1, gg1)
     def da_rows(i):
         rows = slice(512 * i, 512 * i + 512)
         da = jnp.zeros((512, D), f32)
@@ -537,25 +607,21 @@
         for k, j in enumerate(cols if cols is not None else range(first, first + v.shape[1] // 128)):
             dst[pl.ds(j, rows, stride=width), :] = v[0:rows, 128 * k:128 * k + 128]
 
+    w2 = bd[...].reshape(FF, D)
+
     def out_rows(i):
         rows = slice(512 * i, 512 * i + 512)
-        out_v[rows, :] = (hid[rows, :] + dot(act[rows, :], w2[...])).astype(bf16)
+        out_v[rows, :] = (hid[rows, :] + dot(act[rows, :], w2)).astype(bf16)
         copy = pltpu.make_async_copy(out_v.at[rows], out_hbm.at[rows], lsem.at[2 + i])
         copy.start()
         return copy
 
     done = [da_rows(0)]
-    rs_q(2).core_to_near()
-    rs_o.end_far()
-    start(ln_o)
-    rs_q(0).end_far()
-    start(ln_q(0))
+    rs_q[2].core_to_plane()
+    plane_ends(rs_q[1], ln_q[1])
     done.append(da_rows(1))
-    rs_q(1).near_to_far()
     done.append(out_rows(0))
-    rs_q(2).near_to_far()
-    rs_q(1).end_far()
-    start(ln_q(1))
+    plane_ends(rs_q[2], ln_q[2])
     done.append(out_rows(1))
     for j in range(2):
         wait(ln_u[j])
@@ -564,10 +630,8 @@
     from_slot(line_sum(sd, zd), 3, 48, od)
     wait(ln_o)
     from_slot(line_sum(so, zo), 3, 12, oo)
-    rs_q(2).end_far()
-    start(ln_q(2))
     for p in range(PAIRS):
-        wait(ln_q(p))
+        wait(ln_q[p])
         v = line_sum(sq.at[p], zq.at[p])
         from_slot(v, 9, 12, oq, cols=(p, 3 + p, 6 + p))
         if p == 2:
@@ -590,20 +654,25 @@
     scratch = [
         vm((PAIRS,) + BOX + (PAD, D), bf16), vm(BOX + (PAD, D), bf16), vm((2,) + BOX + (PAD, HALF), bf16),
         vm(BOX + (48, D), bf16),
-        vm((D + 32, 512), bf16), vm((D, 3 * D), bf16), vm((D, D), bf16), vm((D, FF), bf16), vm((FF, D), bf16),
+        vm((D + 32, 512), bf16), vm((D, 3 * D), bf16), vm((D, D), bf16), vm((D, FF), bf16),
         vm((8, D), f32), vm((144, 128), f32), vm((PAD, 128), f32),
         vm((T, D), f32), vm((T, 128), f32), vm((T, D), bf16), vm((PAIRS, T, 128), bf16), vm((PAIRS, T, 128), bf16),
         vm((PAIRS, TILES, 128, 256), bf16), vm((T, D), bf16), vm((D, T), bf16), vm((PAIRS, TILES, 8, 256), f32),
-        vm((T, D), f32), vm((T, 128), f32), vm((T, D), bf16), vm((T, FF), bf16), vm((T, HALF), bf16),
-        vm((T, D), f32), vm((T, D), f32), vm((T, D), bf16), vm((T, D), f32), vm((T, D), bf16),
-        vm((PAIRS, TILES, 128, 256), bf16), vm((PAIRS, T, 128), f32), vm((PAIRS, T, 128), f32),
+        vm((T, D), f32), vm((T, 128), f32), vm((T, FF), bf16), vm((T, HALF), bf16),
+        vm((T, D), f32), vm((T, D), f32), vm((T, D), f32), vm((T, D), bf16),
+        vm((PAIRS, TILES, 128, 256), bf16), vm((2, T, 128), f32), vm((2, T, 128), f32),
         vm((PAIRS, T, D), bf16),
         [vm((PAIRS, ke - ks, 256), bf16) for ks, ke in KEYS],
         [vm((ke - ks, 128), f32) for ks, ke in KEYS],
     ]
-    for lead in (BOX, BOX[:4], BOX[:2], BOX[:2], BOX[:1], BOX[:1], (3,)):
-        scratch += [vm(g + lead + s, bf16) for g, s in WIDE]
-    scratch += [dma((8, 2, 8)), dma((8, 2, 8)), dma((4,))]
+    scratch += [vm(BOX + (48, D), bf16)]
+    scratch += [vm(g + BOX[:4] + s, bf16) for g, s in WIDE]
+    scratch += [vm(g + (3, 2, 2) + s, bf16) for g, s in WIDE[:2]]
+    scratch += [vm(g + BOX[:2] + s, bf16) for g, s in WIDE[2:]]
+    for lead in (BOX[:2], BOX[:1], BOX[:1]):
+        scratch += [vm(g + lead + s, bf16) for g, s in WIDE[2:]]
+    scratch += [vm(g + (3,) + s, bf16) for g, s in WIDE]
+    scratch += [vm((T, D), bf16), vm((T, D), bf16), dma((8, 2, 8)), dma((8, 2, 8)), dma((6,))]
     flops = 2 * T * (3 * (3 * D * D + D * D + 2 * D * FF)) + 12 * 2 * 330 * T * D
     return pl.pallas_call(
         layer_kernel,
@@ -616,7 +685,7 @@
             jax.ShapeDtypeStruct(fd.shape, f32),
             jax.ShapeDtypeStruct(fg.shape, f32),
         ],
-        in_specs=[spec] * 8,
+        in_specs=[hbm] + [spec] * 6 + [hbm],
         out_specs=[hbm] * 2 + [spec] * 5,
         scratch_shapes=scratch,
         compiler_params=pltpu.CompilerParams(collective_id=0, has_side_effects=True, vmem_limit_bytes=62 * 2**20),

time: 77.7 us -> 76.6 us (0.986)
  Pallas kernels: 76.7 us -> 75.5 us
    pallas_call x1, Pallas kernels: 73.6 us -> 72.5 us  [layer(): pl.pallas_call(layer_kernel, out_shape=[jax.ShapeDtypeStruct((T, D), bf16...]
where the time goes in v4:
time: 76.6 us; the launch traced here: 76.4 us
  Pallas kernels  75.5 us (99%)
  between operations  0.82 us (1%)
    pallas_call x1, Pallas kernels, layer(): pl.pallas_call(layer_kernel, out_shape=[jax.ShapeDtypeStruct((T, D), bf16...  72.5 us
    pallas_call x1, Pallas kernels, hand_over(): pl.pallas_call(hand_over_kernel, out_shape=[jax.ShapeDtypeStruct(v.shape,...  3.05 us

profile of v4, /device:TPU:0, one launch (start us, length us, event | category | flops | bytes accessed | tf_op | source)
XLA Modules:
  0.0 76.4 jit_solution(9265697589045614375)
XLA Ops:
  0.6 72.5 %layer.1 = (bf16[1024,384]{1,0:T(8,128)(2,1)}, f32[1024,384]{1,0:T(8,128)}, f32[108,128]{1,0:T(8,128)}, f32[36,128]{1,0:T(8,128)}, f32[144,128]{1,0:T(8,128)}, /*index=5*/f32[144,128]{1,0:T(8,128)}, f32[1,24]{1,0:T(1,128)}) custom-call(bf16[1024,384]{1,0:T(8,128)(2,1)} %bitcast.15, s32[1,1024]{1,0:T(1,128)} %seg_ref.1, bf16[108,128]{1,0:T(8,128)(2,1)} %bitcast.23, ...), custom_call_target="tpu_custom_call" | custom-call | flops 13985906688 | bytes 5242880 | tf_op jit(solution)/shard_map/layer/pallas_call | solution.py:677
  73.1 3.0 %hand_over.1 = (bf16[1024,384]{1,0:T(8,128)(2,1)}, f32[1024,384]{1,0:T(8,128)}, f32[108,128]{1,0:T(8,128)}, f32[36,128]{1,0:T(8,128)}, f32[144,128]{1,0:T(8,128)}, /*index=5*/f32[144,128]{1,0:T(8,128)}, f32[1,24]{1,0:T(1,128)}) custom-call(bf16[1024,384]{1,0:T(8,128)(2,1)} %get-tuple-element.21.refs_0_, f32[1024,384]{1,0:T(8,128)} %get-tuple-element.22.refs_1_, ...), custom_call_target="tpu_custom_call" | custom-call | tf_op jit(solution)/shard_map/hand_over/pallas_call | solution.py:721

commit v5 on v4

--- a/solution.py
+++ b/solution.py
@@ -265,7 +265,7 @@
     sf[12:13, 0:24] = fg[...].astype(f32)
     to_slot(fq, 9, 12, lambda j: (bq.at[j % 3], j // 3), (0, 3, 6))
     gq = [[line_of(bq.at[p], gsem.at[p])] + plane_direct(bq.at[p], gsem.at[p]) for p in range(PAIRS)]
-    go = [line_of(bo, gsem.at[3])] + plane_split(bo, gsem.at[3])
+    go = [line_of(bo, gsem.at[3])] + plane_direct(bo, gsem.at[3])
     gu = [[line_of(bu.at[0], gsem.at[4])] + plane_split(bu.at[0], gsem.at[4]), plane_first(bu.at[1], gsem.at[5])]
     gd_line = line_of(bd, gsem.at[6])
     gd = [plane_split(bd, gsem.at[6 + k], pl.ds(k, 1)) for k in range(2)]
@@ -376,10 +376,9 @@
 
     moves = {
         (0, 0): lambda: advance((gq[1], 1), (gu[0], 0)),
-        (0, 6): lambda: (advance((gq[2], 1), (go, 1)), wait(gd_line), start(gd[0][0])),
-        (1, 0): lambda: advance((gu[0], 1)),
+        (0, 6): lambda: (advance((gq[2], 1)), wait(gd_line), start(gd[0][0])),
+        (1, 0): lambda: advance((gu[0], 1), (go, 1)),
         (1, 6): lambda: (advance((gd[0], 0)), start(gd[1][0])),
-        (2, 0): lambda: advance((go, 2)),
         (2, 4): lambda: advance((gu[0], 2)),
         (2, 7): lambda: advance((gd[0], 1)),
     }
@@ -399,7 +398,7 @@
     mix(*last)
 
     get_dy.wait()
-    wait(go[3])
+    wait(go[2])
     wo[...] = dot(u512[0:D, :], bo[...].reshape(512, D)).astype(bf16)
     for i in range(2):
         rows = slice(512 * i, 512 * i + 512)

time: 76.6 us -> 76.2 us (level)
  no operation moved by 1% of the time
where the time goes in v5:
time: 76.2 us; the launch traced here: 76 us
  Pallas kernels  75.2 us (99%)
  between operations  0.82 us (1%)
    pallas_call x1, Pallas kernels, layer(): pl.pallas_call(layer_kernel, out_shape=[jax.ShapeDtypeStruct((T, D), bf16...  72.1 us
    pallas_call x1, Pallas kernels, hand_over(): pl.pallas_call(hand_over_kernel, out_shape=[jax.ShapeDtypeStruct(v.shape,...  3.05 us

profile of v5, /device:TPU:0, one launch (start us, length us, event | category | flops | bytes accessed | tf_op | source)
XLA Modules:
  0.0 76.0 jit_solution(10474664740907029650)
XLA Ops:
  0.6 72.1 %layer.1 = (bf16[1024,384]{1,0:T(8,128)(2,1)}, f32[1024,384]{1,0:T(8,128)}, f32[108,128]{1,0:T(8,128)}, f32[36,128]{1,0:T(8,128)}, f32[144,128]{1,0:T(8,128)}, /*index=5*/f32[144,128]{1,0:T(8,128)}, f32[1,24]{1,0:T(1,128)}) custom-call(bf16[1024,384]{1,0:T(8,128)(2,1)} %bitcast.15, s32[1,1024]{1,0:T(1,128)} %seg_ref.1, bf16[108,128]{1,0:T(8,128)(2,1)} %bitcast.23, ...), custom_call_target="tpu_custom_call" | custom-call | flops 13985906688 | bytes 5242880 | tf_op jit(solution)/shard_map/layer/pallas_call | solution.py:676
  72.8 3.0 %hand_over.1 = (bf16[1024,384]{1,0:T(8,128)(2,1)}, f32[1024,384]{1,0:T(8,128)}, f32[108,128]{1,0:T(8,128)}, f32[36,128]{1,0:T(8,128)}, f32[144,128]{1,0:T(8,128)}, /*index=5*/f32[144,128]{1,0:T(8,128)}, f32[1,24]{1,0:T(1,128)}) custom-call(bf16[1024,384]{1,0:T(8,128)(2,1)} %get-tuple-element.21.refs_0_, f32[1024,384]{1,0:T(8,128)} %get-tuple-element.22.refs_1_, ...), custom_call_target="tpu_custom_call" | custom-call | tf_op jit(solution)/shard_map/hand_over/pallas_call | solution.py:720
